TPU v7x, 512 devices: a whole 4x4x16 slice. The times are simulated.
512 devices in a mesh: gx: 8 (over x, core), gy: 4 (over y), gz: 16 (over z).
Axes of the slice: x: 4, y: 4, z: 16, core: 2. Of those that a mesh axis runs over, the one named last changes fastest.
Arguments:
- rhs: bfloat16 [16, 524288], P(None, ('gx', 'gy', 'gz')), may hold values from -6 to 6
- leaf_basis: bfloat16 [2048, 64, 256], P(('gx', 'gy', 'gz')), may hold values from -0.375 to 0.375
- leaf_transfer: bfloat16 [2048, 64, 64], P(('gx', 'gy', 'gz')), may hold values from -0.375 to 0.375
- leaf_coupling: bfloat16 [2048, 6, 64, 64], P(('gx', 'gy', 'gz')), may hold values from -0.3125 to 0.3125
- coupling_sources: int32 [2048, 6], P(('gx', 'gy', 'gz')), may hold values from -1 to 2047, as said below
- near_tiles: bfloat16 [2048, 3, 256, 256], P(('gx', 'gy', 'gz')), may hold values from -0.21875 to 0.21875
- near_sources: int32 [2048, 3], P(('gx', 'gy', 'gz')), may hold values from -1 to 2047, as said below
- top_transfer: bfloat16 [4, 2, 64, 64], replicated, may hold values from -0.625 to 0.625
- cluster_coupling: bfloat16 [5, 2, 64, 64], replicated, may hold values from -0.5 to 0.5
Outputs:
- product: bfloat16 [16, 524288], P(None, ('gx', 'gy', 'gz'))
Inputs may be any that keep to these rules, and one draw needn't show every extreme that they name: `near_sources`: slot 0 of each leaf is the leaf itself; every other entry is -1 (no block) or a leaf at most 2 places from its target leaf in the global order. `coupling_sources`: each entry is -1 (no block) or a leaf other than the target, at most 2 places from it in the global order.
All inputs are finite; a program needn't handle non-finite values.
Results may differ from a plain program's by a relative error of at most 0.0043.
Values may be sent and summed in bfloat16 or wider, within the bound.
No kernel may reach another device: no remote copies, remote signals or barrier semaphores. Data moves between devices by JAX's collectives and lax.ppermute only.
A program may use at most 64 MiB of HBM per device.

v0:
```python
import jax
import jax.numpy as jnp
from jax import lax
from jax.sharding import PartitionSpec as P

LEAF = 256
NRHS = 16
TOPL = 4


def extended(cells, sides, width):
    for axis, dim in sides:
        count = lax.axis_size(axis)
        ends = count - 1
        head = lax.slice_in_dim(cells, 0, width, axis=dim)
        tail = lax.slice_in_dim(cells, cells.shape[dim] - width, cells.shape[dim], axis=dim)
        cells = jnp.concatenate(
            [
                lax.ppermute(tail, axis, [(i, (i + 1) % count) for i in range(ends)]),
                cells,
                lax.ppermute(head, axis, [((i + 1) % count, i) for i in range(ends)]),
            ],
            axis=dim,
        )
    return cells


def swapped(shard, axis, stride):
    return lax.ppermute(shard, axis, [(i, i ^ 1 << stride) for i in range(lax.axis_size(axis))])


def passed_along(block, axis, distance):
    devices = range(lax.axis_size(axis))
    route = [(i - distance, i) for i in devices if i - distance in devices]
    return lax.ppermute(block, axis, route)


def parity_matrix(mats, parity, flipped):
    first = mats[0]
    second = mats[1]
    if flipped:
        return jnp.where(parity == 0, second, first)
    return jnp.where(parity == 0, first, second)


def local(
    rhs,
    leaf_basis,
    leaf_transfer,
    leaf_coupling,
    coupling_sources,
    near_tiles,
    near_sources,
    top_transfer,
    cluster_coupling,
):
    exact = lax.Precision.HIGHEST
    dev_index = lax.axis_index(("gx", "gy", "gz"))
    leaf_count = leaf_basis.shape[0]
    span = leaf_count + 2 * leaf_count
    anchor = dev_index * leaf_count - leaf_count

    def local_pick(wide, sources, axis_at):
        position = jnp.clip(sources - anchor, 0, span - 1)
        return (jnp.take(wide, position, axis=axis_at), sources >= 0)

    wide_rhs = extended(rhs, ((("gx", "gy", "gz"), 1),), leaf_count * LEAF)
    wide_rhs = wide_rhs.reshape(NRHS, span, LEAF)
    blocks = rhs.reshape(NRHS, leaf_count, LEAF)
    coeffs = jnp.einsum(
        "rts,tks->trk", blocks, leaf_basis, preferred_element_type=jnp.float32
    ).astype(jnp.bfloat16)
    coeff_wide = extended(coeffs, ((("gx", "gy", "gz"), 0),), leaf_count)
    picked, usable = local_pick(coeff_wide, coupling_sources, 0)
    picked = jnp.where(usable[:, :, None, None], picked, jnp.zeros((), jnp.bfloat16))
    leaf_field = jnp.einsum(
        "tark,takm->trm", picked, leaf_coupling, preferred_element_type=jnp.float32
    )
    root_coeff = jnp.einsum(
        "trk,tkm->rm", coeffs, leaf_transfer, preferred_element_type=jnp.float32
    )
    up_mats = top_transfer.astype(jnp.float32)
    coupling_mats = cluster_coupling.astype(jnp.float32)
    fields = []
    climbed = [root_coeff]
    for height in range(1, TOPL + 1):
        partner = swapped(climbed[-1], ("gx", "gy", "gz"), height - 1)
        parity = dev_index >> height - 1 & 1
        own_mat = parity_matrix(up_mats[height - 1], parity, False)
        other_mat = parity_matrix(up_mats[height - 1], parity, True)
        climbed.append(
            jnp.dot(climbed[-1], own_mat, precision=exact)
            + jnp.dot(partner, other_mat, precision=exact)
        )
    for height in range(TOPL + 1):
        stride = 2**height
        lower_side = passed_along(climbed[height], ("gx", "gy", "gz"), stride)
        upper_side = passed_along(climbed[height], ("gx", "gy", "gz"), -stride)
        fields.append(
            jnp.dot(lower_side, coupling_mats[height, 0], precision=exact)
            + jnp.dot(upper_side, coupling_mats[height, 1], precision=exact)
        )
    incoming = fields[TOPL]
    for height in range(TOPL, 0, -1):
        parity = dev_index >> height - 1 & 1
        own_mat = parity_matrix(up_mats[height - 1], parity, False)
        incoming = fields[height - 1] + jnp.dot(incoming, own_mat.T, precision=exact)
    spread = jnp.einsum("rm,tkm->trk", incoming, leaf_transfer.astype(jnp.float32), precision=exact)
    potential = (leaf_field + spread).astype(jnp.bfloat16)
    far_part = jnp.einsum("trk,tks->rts", potential, leaf_basis, preferred_element_type=jnp.float32)
    near_in, near_ok = local_pick(wide_rhs, near_sources, 1)
    near_in = jnp.where(near_ok[None, :, :, None], near_in, jnp.zeros((), jnp.bfloat16))
    near_part = jnp.einsum(
        "rtns,tnsu->rtu", near_in, near_tiles, preferred_element_type=jnp.float32
    )
    return (far_part + near_part).reshape(NRHS, leaf_count * LEAF).astype(jnp.bfloat16)


def solution(mesh):
    placed = (
        P(None, ("gx", "gy", "gz")),
        P(("gx", "gy", "gz"), None, None),
        P(("gx", "gy", "gz"), None, None),
        P(("gx", "gy", "gz"), None, None, None),
        P(("gx", "gy", "gz"), None),
        P(("gx", "gy", "gz"), None, None, None),
        P(("gx", "gy", "gz"), None),
        P(),
        P(),
    )
    return jax.shard_map(
        local, mesh=mesh, in_specs=placed, out_specs=P(None, ("gx", "gy", "gz")), check_vma=False
    )
```

profile of v0, /device:TPU:6, one launch (start us, length us, event | category | flops | bytes accessed | tf_op | source)
XLA Modules:
  0.0 147.3 jit_solution(12047381120401837559)
XLA Ops:
  0.0 1.2 convolution_convert_fusion
  1.2 1.0 convolution_bitcast_fusion.3
  2.3 3.8 %collective-permute-start.4 = (f32[16,64]{1,0:T(8,128)S(1)}, f32[16,64]{1,0:T(8,128)S(1)}, u32[]{:S(2)}, u32[]{:S(2)}) collective-permute-start(f32[16,64]{1,0:T(8,128)S(1)} %convolution_bitcast_fusion.3), channel_id=1, source_target_pairs={{0,1},{1,0},{2,3},{3,2},{4,5},{5,4},{6,7},{7,6},{8,9},{9,8},{10,11... | collective-permute-start | bytes 12296 | tf_op jit(solution)/shard_map/ppermute | solution.py:29
  6.1 12.4 %collective-permute-start.3 = (f32[16,64]{1,0:T(8,128)S(1)}, f32[16,64]{1,0:T(8,128)S(1)}, u32[]{:S(2)}, u32[]{:S(2)}) collective-permute-start(f32[16,64]{1,0:T(8,128)S(1)} %convolution_bitcast_fusion.3), channel_id=1, source_target_pairs={{1,0},{2,1},{3,2},{4,3},{5,4},{6,5},{7,6},{8,7},{9,8},{10,9},{11,1... | collective-permute-start | bytes 12296 | tf_op jit(solution)/shard_map/ppermute | solution.py:35
  18.5 1.9 %collective-permute-start.2 = (f32[16,64]{1,0:T(8,128)S(1)}, f32[16,64]{1,0:T(8,128)S(1)}, u32[]{:S(2)}, u32[]{:S(2)}) collective-permute-start(f32[16,64]{1,0:T(8,128)S(1)} %convolution_bitcast_fusion.3), channel_id=1, source_target_pairs={{0,1},{1,2},{2,3},{3,4},{4,5},{5,6},{6,7},{7,8},{8,9},{9,10},{10,1... | collective-permute-start | bytes 12296 | tf_op jit(solution)/shard_map/ppermute | solution.py:35
  20.4 1.9 %collective-permute-start = (bf16[4,16,64]{2,1,0:T(8,128)(2,1)S(1)}, bf16[4,16,64]{2,1,0:T(8,128)(2,1)S(1)}, u32[]{:S(2)}, u32[]{:S(2)}) collective-permute-start(bf16[4,16,64]{2,1,0:T(8,128)(2,1)S(1)} %convolution_convert_fusion), channel_id=1, source_target_pairs={{0,1},{1,2},{2,3},{3,4},{4,5},{5,6},{6,7},{7,8},{8,9},{9,10},{10,1... | collective-permute-start | bytes 24584 | tf_op jit(solution)/shard_map/ppermute | solution.py:19
  22.3 7.9 %collective-permute-start.1 = (bf16[4,16,64]{2,1,0:T(8,128)(2,1)S(1)}, bf16[4,16,64]{2,1,0:T(8,128)(2,1)S(1)}, u32[]{:S(2)}, u32[]{:S(2)}) collective-permute-start(bf16[4,16,64]{2,1,0:T(8,128)(2,1)S(1)} %convolution_convert_fusion), channel_id=1, source_target_pairs={{1,0},{2,1},{3,2},{4,3},{5,4},{6,5},{7,6},{8,7},{9,8},{10,9},{11,1... | collective-permute-start | bytes 24584 | tf_op jit(solution)/shard_map/ppermute | solution.py:21
  30.2 0.9 convert_element_type.21
  32.9 1.9 %collective-permute-start.16 = (bf16[16,1024]{1,0:T(8,128)(2,1)}, bf16[16,1024]{1,0:T(8,128)(2,1)S(1)}, u32[]{:S(2)}, u32[]{:S(2)}) collective-permute-start(bf16[16,1024]{1,0:T(8,128)(2,1)} %param.9), channel_id=1, source_target_pairs={{0,1},{1,2},{2,3},{3,4},{4,5},{5,6},{6,7},{7,8},{8,9},{9,10},{10,1... | collective-permute-start | bytes 98312 | tf_op jit(solution)/shard_map/ppermute | solution.py:19
  35.1 1.9 %collective-permute-start.7 = (f32[16,64]{1,0:T(8,128)S(1)}, f32[16,64]{1,0:T(8,128)S(1)}, u32[]{:S(2)}, u32[]{:S(2)}) collective-permute-start(f32[16,64]{1,0:T(8,128)S(1)} %convolution_add_fusion.7), channel_id=1, source_target_pairs={{0,2},{1,3},{2,0},{3,1},{4,6},{5,7},{6,4},{7,5},{8,10},{9,11},{10,... | collective-permute-start | bytes 12296 | tf_op jit(solution)/shard_map/ppermute | solution.py:29
  37.0 0.8 fusion.69
  37.9 3.7 %collective-permute-done.7 = f32[16,64]{1,0:T(8,128)S(1)} collective-permute-done((f32[16,64]{1,0:T(8,128)S(1)}, f32[16,64]{1,0:T(8,128)S(1)}, u32[]{:S(2)}, u32[]{:S(2)}) %collective-permute-start.7) | collective-permute-done | bytes 4128 | tf_op jit(solution)/shard_map/ppermute | solution.py:29
  41.6 6.7 %collective-permute-start.17 = (bf16[16,1024]{1,0:T(8,128)(2,1)}, bf16[16,1024]{1,0:T(8,128)(2,1)S(1)}, u32[]{:S(2)}, u32[]{:S(2)}) collective-permute-start(bf16[16,1024]{1,0:T(8,128)(2,1)} %param.9), channel_id=1, source_target_pairs={{1,0},{2,1},{3,2},{4,3},{5,4},{6,5},{7,6},{8,7},{9,8},{10,9},{11,1... | collective-permute-start | bytes 98312 | tf_op jit(solution)/shard_map/ppermute | solution.py:21
  48.6 1.9 %collective-permute-start.6 = (f32[16,64]{1,0:T(8,128)S(1)}, f32[16,64]{1,0:T(8,128)S(1)}, u32[]{:S(2)}, u32[]{:S(2)}) collective-permute-start(f32[16,64]{1,0:T(8,128)S(1)} %convolution_add_fusion.7), channel_id=1, source_target_pairs={{2,0},{3,1},{4,2},{5,3},{6,4},{7,5},{8,6},{9,7},{10,8},{11,9},{12,... | collective-permute-start | bytes 12296 | tf_op jit(solution)/shard_map/ppermute | solution.py:35
  50.5 4.8 %collective-permute-start.5 = (f32[16,64]{1,0:T(8,128)S(1)}, f32[16,64]{1,0:T(8,128)S(1)}, u32[]{:S(2)}, u32[]{:S(2)}) collective-permute-start(f32[16,64]{1,0:T(8,128)S(1)} %convolution_add_fusion.7), channel_id=1, source_target_pairs={{0,2},{1,3},{2,4},{3,5},{4,6},{5,7},{6,8},{7,9},{8,10},{9,11},{10,... | collective-permute-start | bytes 12296 | tf_op jit(solution)/shard_map/ppermute | solution.py:35
  56.0 1.9 %collective-permute-start.10 = (f32[16,64]{1,0:T(8,128)S(1)}, f32[16,64]{1,0:T(8,128)S(1)}, u32[]{:S(2)}, u32[]{:S(2)}) collective-permute-start(f32[16,64]{1,0:T(8,128)S(1)} %convolution_add_fusion.5), channel_id=1, source_target_pairs={{0,4},{1,5},{2,6},{3,7},{4,0},{5,1},{6,2},{7,3},{8,12},{9,13},{10,... | collective-permute-start | bytes 12296 | tf_op jit(solution)/shard_map/ppermute | solution.py:29
  58.7 1.3 convolution_bitcast_fusion.2
  60.1 5.3 %collective-permute-done.10 = f32[16,64]{1,0:T(8,128)S(1)} collective-permute-done((f32[16,64]{1,0:T(8,128)S(1)}, f32[16,64]{1,0:T(8,128)S(1)}, u32[]{:S(2)}, u32[]{:S(2)}) %collective-permute-start.10) | collective-permute-done | bytes 4128 | tf_op jit(solution)/shard_map/ppermute | solution.py:29
  65.4 1.9 %collective-permute-start.9 = (f32[16,64]{1,0:T(8,128)S(1)}, f32[16,64]{1,0:T(8,128)S(1)}, u32[]{:S(2)}, u32[]{:S(2)}) collective-permute-start(f32[16,64]{1,0:T(8,128)S(1)} %convolution_add_fusion.5), channel_id=1, source_target_pairs={{4,0},{5,1},{6,2},{7,3},{8,4},{9,5},{10,6},{11,7},{12,8},{13,9},{1... | collective-permute-start | bytes 12296 | tf_op jit(solution)/shard_map/ppermute | solution.py:35
  67.6 7.2 %collective-permute-done.9 = f32[16,64]{1,0:T(8,128)S(1)} collective-permute-done((f32[16,64]{1,0:T(8,128)S(1)}, f32[16,64]{1,0:T(8,128)S(1)}, u32[]{:S(2)}, u32[]{:S(2)}) %collective-permute-start.9) | collective-permute-done | bytes 4128 | tf_op jit(solution)/shard_map/ppermute | solution.py:35
  74.9 2.1 %collective-permute-start.13 = (f32[16,64]{1,0:T(8,128)S(1)}, f32[16,64]{1,0:T(8,128)S(1)}, u32[]{:S(2)}, u32[]{:S(2)}) collective-permute-start(f32[16,64]{1,0:T(8,128)S(1)} %convolution_add_fusion.3), channel_id=1, source_target_pairs={{0,8},{1,9},{2,10},{3,11},{4,12},{5,13},{6,14},{7,15},{8,0},{9,1},... | collective-permute-start | bytes 12296 | tf_op jit(solution)/shard_map/ppermute | solution.py:29
  77.0 12.0 %collective-permute-done.13 = f32[16,64]{1,0:T(8,128)S(1)} collective-permute-done((f32[16,64]{1,0:T(8,128)S(1)}, f32[16,64]{1,0:T(8,128)S(1)}, u32[]{:S(2)}, u32[]{:S(2)}) %collective-permute-start.13) | collective-permute-done | bytes 4128 | tf_op jit(solution)/shard_map/ppermute | solution.py:29
  89.1 1.9 %collective-permute-start.12 = (f32[16,64]{1,0:T(8,128)S(1)}, f32[16,64]{1,0:T(8,128)S(1)}, u32[]{:S(2)}, u32[]{:S(2)}) collective-permute-start(f32[16,64]{1,0:T(8,128)S(1)} %convolution_add_fusion.3), channel_id=1, source_target_pairs={{8,0},{9,1},{10,2},{11,3},{12,4},{13,5},{14,6},{15,7},{16,8},{17,9... | collective-permute-start | bytes 12296 | tf_op jit(solution)/shard_map/ppermute | solution.py:35
  91.2 12.2 %collective-permute-done.12 = f32[16,64]{1,0:T(8,128)S(1)} collective-permute-done((f32[16,64]{1,0:T(8,128)S(1)}, f32[16,64]{1,0:T(8,128)S(1)}, u32[]{:S(2)}, u32[]{:S(2)}) %collective-permute-start.12) | collective-permute-done | bytes 4128 | tf_op jit(solution)/shard_map/ppermute | solution.py:35
  103.3 1.9 %collective-permute-start.15 = (f32[16,64]{1,0:T(8,128)S(1)}, f32[16,64]{1,0:T(8,128)S(1)}, u32[]{:S(2)}, u32[]{:S(2)}) collective-permute-start(f32[16,64]{1,0:T(8,128)S(1)} %convolution_add_fusion.1), channel_id=1, source_target_pairs={{16,0},{17,1},{18,2},{19,3},{20,4},{21,5},{22,6},{23,7},{24,8},{25... | collective-permute-start | bytes 12296 | tf_op jit(solution)/shard_map/ppermute | solution.py:35
  105.4 3.5 %collective-permute-done.15 = f32[16,64]{1,0:T(8,128)S(1)} collective-permute-done((f32[16,64]{1,0:T(8,128)S(1)}, f32[16,64]{1,0:T(8,128)S(1)}, u32[]{:S(2)}, u32[]{:S(2)}) %collective-permute-start.15) | collective-permute-done | bytes 4128 | tf_op jit(solution)/shard_map/ppermute | solution.py:35
  108.9 1.9 %collective-permute-start.14 = (f32[16,64]{1,0:T(8,128)S(1)}, f32[16,64]{1,0:T(8,128)S(1)}, u32[]{:S(2)}, u32[]{:S(2)}) collective-permute-start(f32[16,64]{1,0:T(8,128)S(1)} %convolution_add_fusion.1), channel_id=1, source_target_pairs={{0,16},{1,17},{2,18},{3,19},{4,20},{5,21},{6,22},{7,23},{8,24},{9,... | collective-permute-start | bytes 12296 | tf_op jit(solution)/shard_map/ppermute | solution.py:35
  110.9 5.0 %collective-permute-done.14 = f32[16,64]{1,0:T(8,128)S(1)} collective-permute-done((f32[16,64]{1,0:T(8,128)S(1)}, f32[16,64]{1,0:T(8,128)S(1)}, u32[]{:S(2)}, u32[]{:S(2)}) %collective-permute-start.14) | collective-permute-done | bytes 4128 | tf_op jit(solution)/shard_map/ppermute | solution.py:35
  115.9 3.0 %collective-permute-start.11 = (f32[16,64]{1,0:T(8,128)S(1)}, f32[16,64]{1,0:T(8,128)S(1)}, u32[]{:S(2)}, u32[]{:S(2)}) collective-permute-start(f32[16,64]{1,0:T(8,128)S(1)} %convolution_add_fusion.3), channel_id=1, source_target_pairs={{0,8},{1,9},{2,10},{3,11},{4,12},{5,13},{6,14},{7,15},{8,16},{9,17... | collective-permute-start | bytes 12296 | tf_op jit(solution)/shard_map/ppermute | solution.py:35
  119.2 13.4 %collective-permute-done.11 = f32[16,64]{1,0:T(8,128)S(1)} collective-permute-done((f32[16,64]{1,0:T(8,128)S(1)}, f32[16,64]{1,0:T(8,128)S(1)}, u32[]{:S(2)}, u32[]{:S(2)}) %collective-permute-start.11) | collective-permute-done | bytes 4128 | tf_op jit(solution)/shard_map/ppermute | solution.py:35
  132.6 2.5 %collective-permute-start.8 = (f32[16,64]{1,0:T(8,128)S(1)}, f32[16,64]{1,0:T(8,128)S(1)}, u32[]{:S(2)}, u32[]{:S(2)}) collective-permute-start(f32[16,64]{1,0:T(8,128)S(1)} %convolution_add_fusion.5), channel_id=1, source_target_pairs={{0,4},{1,5},{2,6},{3,7},{4,8},{5,9},{6,10},{7,11},{8,12},{9,13},{1... | collective-permute-start | bytes 12296 | tf_op jit(solution)/shard_map/ppermute | solution.py:35
  135.4 9.1 %collective-permute-done.8 = f32[16,64]{1,0:T(8,128)S(1)} collective-permute-done((f32[16,64]{1,0:T(8,128)S(1)}, f32[16,64]{1,0:T(8,128)S(1)}, u32[]{:S(2)}, u32[]{:S(2)}) %collective-permute-start.8) | collective-permute-done | bytes 4128 | tf_op jit(solution)/shard_map/ppermute | solution.py:35
  (55 shorter events, 7.8 us)
Async XLA Ops:
  0.0 146.3 %copy-start = (bf16[4,3,256,256]{3,2,1,0:T(8,128)(2,1)S(1)}, bf16[4,3,256,256]{3,2,1,0:T(8,128)(2,1)}, u32[]{:S(2)}) copy-start(bf16[4,3,256,256]{3,2,1,0:T(8,128)(2,1)} %param.14) | copy-start | bytes 4718596
  0.0 145.7 %copy-start.4 = (bf16[16,1024]{1,0:T(8,128)(2,1)S(1)}, bf16[16,1024]{1,0:T(8,128)(2,1)}, u32[]{:S(2)}) copy-start(bf16[16,1024]{1,0:T(8,128)(2,1)} %param.9) | copy-start | bytes 98308
  0.0 145.5 %copy-start.1 = (bf16[4,64,256]{2,1,0:T(8,128)(2,1)S(1)}, bf16[4,64,256]{2,1,0:T(8,128)(2,1)}, u32[]{:S(2)}) copy-start(bf16[4,64,256]{2,1,0:T(8,128)(2,1)} %param.10) | copy-start | bytes 393220
  0.0 145.3 %copy-start.2 = (bf16[4,64,64]{2,1,0:T(8,128)(2,1)S(1)}, bf16[4,64,64]{2,1,0:T(8,128)(2,1)}, u32[]{:S(2)}) copy-start(bf16[4,64,64]{2,1,0:T(8,128)(2,1)} %param.11) | copy-start | bytes 98308
  0.0 76.9 %copy-start.3 = (bf16[5,2,64,64]{3,2,1,0:T(8,128)(2,1)S(1)}, bf16[5,2,64,64]{3,2,1,0:T(8,128)(2,1)}, u32[]{:S(2)}) copy-start(bf16[5,2,64,64]{3,2,1,0:T(8,128)(2,1)} %param.17) | copy-start | bytes 245764
  2.3 30.6 %collective-permute-start.4 = (f32[16,64]{1,0:T(8,128)S(1)}, f32[16,64]{1,0:T(8,128)S(1)}, u32[]{:S(2)}, u32[]{:S(2)}) collective-permute-start(f32[16,64]{1,0:T(8,128)S(1)} %convolution_bitcast_fusion.3), channel_id=1, source_target_pairs={{0,1},{1,0},{2,3},{3,2},{4,5},{5,4},{6,7},{7,6},{8,9},{9,8},{10,11... | collective-permute-start | bytes 12296 | tf_op jit(solution)/shard_map/ppermute | solution.py:29
  6.1 29.0 %collective-permute-start.3 = (f32[16,64]{1,0:T(8,128)S(1)}, f32[16,64]{1,0:T(8,128)S(1)}, u32[]{:S(2)}, u32[]{:S(2)}) collective-permute-start(f32[16,64]{1,0:T(8,128)S(1)} %convolution_bitcast_fusion.3), channel_id=1, source_target_pairs={{1,0},{2,1},{3,2},{4,3},{5,4},{6,5},{7,6},{8,7},{9,8},{10,9},{11,1... | collective-permute-start | bytes 12296 | tf_op jit(solution)/shard_map/ppermute | solution.py:35
  18.5 126.7 %collective-permute-start.2 = (f32[16,64]{1,0:T(8,128)S(1)}, f32[16,64]{1,0:T(8,128)S(1)}, u32[]{:S(2)}, u32[]{:S(2)}) collective-permute-start(f32[16,64]{1,0:T(8,128)S(1)} %convolution_bitcast_fusion.3), channel_id=1, source_target_pairs={{0,1},{1,2},{2,3},{3,4},{4,5},{5,6},{6,7},{7,8},{8,9},{9,10},{10,1... | collective-permute-start | bytes 12296 | tf_op jit(solution)/shard_map/ppermute | solution.py:35
  20.4 28.2 %collective-permute-start = (bf16[4,16,64]{2,1,0:T(8,128)(2,1)S(1)}, bf16[4,16,64]{2,1,0:T(8,128)(2,1)S(1)}, u32[]{:S(2)}, u32[]{:S(2)}) collective-permute-start(bf16[4,16,64]{2,1,0:T(8,128)(2,1)S(1)} %convolution_convert_fusion), channel_id=1, source_target_pairs={{0,1},{1,2},{2,3},{3,4},{4,5},{5,6},{6,7},{7,8},{8,9},{9,10},{10,1... | collective-permute-start | bytes 24584 | tf_op jit(solution)/shard_map/ppermute | solution.py:19
  22.3 28.2 %collective-permute-start.1 = (bf16[4,16,64]{2,1,0:T(8,128)(2,1)S(1)}, bf16[4,16,64]{2,1,0:T(8,128)(2,1)S(1)}, u32[]{:S(2)}, u32[]{:S(2)}) collective-permute-start(bf16[4,16,64]{2,1,0:T(8,128)(2,1)S(1)} %convolution_convert_fusion), channel_id=1, source_target_pairs={{1,0},{2,1},{3,2},{4,3},{5,4},{6,5},{7,6},{8,7},{9,8},{10,9},{11,1... | collective-permute-start | bytes 24584 | tf_op jit(solution)/shard_map/ppermute | solution.py:21
  32.9 112.8 %collective-permute-start.16 = (bf16[16,1024]{1,0:T(8,128)(2,1)}, bf16[16,1024]{1,0:T(8,128)(2,1)S(1)}, u32[]{:S(2)}, u32[]{:S(2)}) collective-permute-start(bf16[16,1024]{1,0:T(8,128)(2,1)} %param.9), channel_id=1, source_target_pairs={{0,1},{1,2},{2,3},{3,4},{4,5},{5,6},{6,7},{7,8},{8,9},{9,10},{10,1... | collective-permute-start | bytes 98312 | tf_op jit(solution)/shard_map/ppermute | solution.py:19
  35.1 6.4 %collective-permute-start.7 = (f32[16,64]{1,0:T(8,128)S(1)}, f32[16,64]{1,0:T(8,128)S(1)}, u32[]{:S(2)}, u32[]{:S(2)}) collective-permute-start(f32[16,64]{1,0:T(8,128)S(1)} %convolution_add_fusion.7), channel_id=1, source_target_pairs={{0,2},{1,3},{2,0},{3,1},{4,6},{5,7},{6,4},{7,5},{8,10},{9,11},{10,... | collective-permute-start | bytes 12296 | tf_op jit(solution)/shard_map/ppermute | solution.py:29
  41.6 104.1 %collective-permute-start.17 = (bf16[16,1024]{1,0:T(8,128)(2,1)}, bf16[16,1024]{1,0:T(8,128)(2,1)S(1)}, u32[]{:S(2)}, u32[]{:S(2)}) collective-permute-start(bf16[16,1024]{1,0:T(8,128)(2,1)} %param.9), channel_id=1, source_target_pairs={{1,0},{2,1},{3,2},{4,3},{5,4},{6,5},{7,6},{8,7},{9,8},{10,9},{11,1... | collective-permute-start | bytes 98312 | tf_op jit(solution)/shard_map/ppermute | solution.py:21
  48.6 7.4 %collective-permute-start.6 = (f32[16,64]{1,0:T(8,128)S(1)}, f32[16,64]{1,0:T(8,128)S(1)}, u32[]{:S(2)}, u32[]{:S(2)}) collective-permute-start(f32[16,64]{1,0:T(8,128)S(1)} %convolution_add_fusion.7), channel_id=1, source_target_pairs={{2,0},{3,1},{4,2},{5,3},{6,4},{7,5},{8,6},{9,7},{10,8},{11,9},{12,... | collective-permute-start | bytes 12296 | tf_op jit(solution)/shard_map/ppermute | solution.py:35
  50.5 94.3 %collective-permute-start.5 = (f32[16,64]{1,0:T(8,128)S(1)}, f32[16,64]{1,0:T(8,128)S(1)}, u32[]{:S(2)}, u32[]{:S(2)}) collective-permute-start(f32[16,64]{1,0:T(8,128)S(1)} %convolution_add_fusion.7), channel_id=1, source_target_pairs={{0,2},{1,3},{2,4},{3,5},{4,6},{5,7},{6,8},{7,9},{8,10},{9,11},{10,... | collective-permute-start | bytes 12296 | tf_op jit(solution)/shard_map/ppermute | solution.py:35
  56.0 9.5 %collective-permute-start.10 = (f32[16,64]{1,0:T(8,128)S(1)}, f32[16,64]{1,0:T(8,128)S(1)}, u32[]{:S(2)}, u32[]{:S(2)}) collective-permute-start(f32[16,64]{1,0:T(8,128)S(1)} %convolution_add_fusion.5), channel_id=1, source_target_pairs={{0,4},{1,5},{2,6},{3,7},{4,0},{5,1},{6,2},{7,3},{8,12},{9,13},{10,... | collective-permute-start | bytes 12296 | tf_op jit(solution)/shard_map/ppermute | solution.py:29
  65.4 9.4 %collective-permute-start.9 = (f32[16,64]{1,0:T(8,128)S(1)}, f32[16,64]{1,0:T(8,128)S(1)}, u32[]{:S(2)}, u32[]{:S(2)}) collective-permute-start(f32[16,64]{1,0:T(8,128)S(1)} %convolution_add_fusion.5), channel_id=1, source_target_pairs={{4,0},{5,1},{6,2},{7,3},{8,4},{9,5},{10,6},{11,7},{12,8},{13,9},{1... | collective-permute-start | bytes 12296 | tf_op jit(solution)/shard_map/ppermute | solution.py:35
  74.9 14.2 %collective-permute-start.13 = (f32[16,64]{1,0:T(8,128)S(1)}, f32[16,64]{1,0:T(8,128)S(1)}, u32[]{:S(2)}, u32[]{:S(2)}) collective-permute-start(f32[16,64]{1,0:T(8,128)S(1)} %convolution_add_fusion.3), channel_id=1, source_target_pairs={{0,8},{1,9},{2,10},{3,11},{4,12},{5,13},{6,14},{7,15},{8,0},{9,1},... | collective-permute-start | bytes 12296 | tf_op jit(solution)/shard_map/ppermute | solution.py:29
  89.1 14.2 %collective-permute-start.12 = (f32[16,64]{1,0:T(8,128)S(1)}, f32[16,64]{1,0:T(8,128)S(1)}, u32[]{:S(2)}, u32[]{:S(2)}) collective-permute-start(f32[16,64]{1,0:T(8,128)S(1)} %convolution_add_fusion.3), channel_id=1, source_target_pairs={{8,0},{9,1},{10,2},{11,3},{12,4},{13,5},{14,6},{15,7},{16,8},{17,9... | collective-permute-start | bytes 12296 | tf_op jit(solution)/shard_map/ppermute | solution.py:35
  103.3 5.5 %collective-permute-start.15 = (f32[16,64]{1,0:T(8,128)S(1)}, f32[16,64]{1,0:T(8,128)S(1)}, u32[]{:S(2)}, u32[]{:S(2)}) collective-permute-start(f32[16,64]{1,0:T(8,128)S(1)} %convolution_add_fusion.1), channel_id=1, source_target_pairs={{16,0},{17,1},{18,2},{19,3},{20,4},{21,5},{22,6},{23,7},{24,8},{25... | collective-permute-start | bytes 12296 | tf_op jit(solution)/shard_map/ppermute | solution.py:35
  108.9 7.1 %collective-permute-start.14 = (f32[16,64]{1,0:T(8,128)S(1)}, f32[16,64]{1,0:T(8,128)S(1)}, u32[]{:S(2)}, u32[]{:S(2)}) collective-permute-start(f32[16,64]{1,0:T(8,128)S(1)} %convolution_add_fusion.1), channel_id=1, source_target_pairs={{0,16},{1,17},{2,18},{3,19},{4,20},{5,21},{6,22},{7,23},{8,24},{9,... | collective-permute-start | bytes 12296 | tf_op jit(solution)/shard_map/ppermute | solution.py:35
  115.9 16.7 %collective-permute-start.11 = (f32[16,64]{1,0:T(8,128)S(1)}, f32[16,64]{1,0:T(8,128)S(1)}, u32[]{:S(2)}, u32[]{:S(2)}) collective-permute-start(f32[16,64]{1,0:T(8,128)S(1)} %convolution_add_fusion.3), channel_id=1, source_target_pairs={{0,8},{1,9},{2,10},{3,11},{4,12},{5,13},{6,14},{7,15},{8,16},{9,17... | collective-permute-start | bytes 12296 | tf_op jit(solution)/shard_map/ppermute | solution.py:35
  132.6 11.9 %collective-permute-start.8 = (f32[16,64]{1,0:T(8,128)S(1)}, f32[16,64]{1,0:T(8,128)S(1)}, u32[]{:S(2)}, u32[]{:S(2)}) collective-permute-start(f32[16,64]{1,0:T(8,128)S(1)} %convolution_add_fusion.5), channel_id=1, source_target_pairs={{0,4},{1,5},{2,6},{3,7},{4,8},{5,9},{6,10},{7,11},{8,12},{9,13},{1... | collective-permute-start | bytes 12296 | tf_op jit(solution)/shard_map/ppermute | solution.py:35
where the time goes:
time: 148 us; the launch traced here: 147 us
  waiting for transfers between devices  71.6 us (48%)
  starting transfers between devices  62.3 us (42%)
  matrix products  8.74 us (6%)
  other arithmetic  2.36 us (2%)
  local copies, waits for them, and re-layouts  1.96 us (1%)
    ppermute x10, waiting for transfers between devices, passed_along(): return lax.ppermute(block, axis, route)  50.5 us
    ppermute x10, starting transfers between devices, passed_along(): return lax.ppermute(block, axis, route)  34.1 us
    ppermute x4, waiting for transfers between devices, swapped(): lax.ppermute(shard, axis, [(i, i ^ 1 << stride) for i in range(lax.axis_s...  21.1 us
    ppermute x2, starting transfers between devices, extended(): lax.ppermute(head, axis, [((i + 1) % count, i) for i in range(ends)])  14.6 us
    ppermute x4, starting transfers between devices, swapped(): lax.ppermute(shard, axis, [(i, i ^ 1 << stride) for i in range(lax.axis_s...  9.72 us
    ppermute x2, starting transfers between devices, extended(): lax.ppermute(tail, axis, [(i, (i + 1) % count) for i in range(ends)])  3.84 us
  transfers between devices with their start and end apart: 18, of which 9 were waited for; matrix products, arithmetic and copies ran while one was open for 6% of the time, Pallas kernels for 0%

commit v1 on v0

v1 whole, which is shorter than its diff:
```python
import jax
import jax.numpy as jnp
from jax import lax
from jax.experimental import pallas as pl
from jax.experimental.pallas import tpu as pltpu
from jax.sharding import PartitionSpec as P

LEAF = 256
RANK = 64
NRHS = 16
NEAR = 3
ADM = 6
TOPL = 4
LEAF_DEV = 4
REACH = 2
LINE = 16
LEADER = 11
AXES = ("gx", "gy", "gz")
EDGE = REACH * (LEAF + RANK)
VMEM = pl.BlockSpec(memory_space=pltpu.VMEM)
SMEM = pl.BlockSpec(memory_space=pltpu.SMEM)
HBM = pl.BlockSpec(memory_space=pltpu.HBM)
STAGED = 9
NT = (((1,), (1,)), ((), ()))
NN = (((1,), (0,)), ((), ()))


def dot(a, b, dims=NN):
    return lax.dot_general(a, b, dims, preferred_element_type=jnp.float32)


def dot_split(a, b, dims=NN):
    high = a.astype(jnp.bfloat16)
    low = (a - high.astype(jnp.float32)).astype(jnp.bfloat16)
    both = dot(jnp.concatenate([high, low], 0), b, dims)
    return both[: a.shape[0]] + both[a.shape[0] :]


def coeff_kernel(*refs):
    staged, coeffs_ref, sends_ref, tail_ref, head_ref = refs[:STAGED], *refs[STAGED : STAGED + 4]
    kept, done = refs[STAGED + 4 : -1], refs[-1]
    copies = [
        pltpu.make_async_copy(staged[i], kept[i], done.at[i]) for i in range(STAGED)
    ]
    for copy in copies:
        copy.start()
    rhs_ref, basis_ref, transfer_ref = kept[:3]
    copies[0].wait()
    wide = REACH * LEAF
    tail_ref[:, :wide] = rhs_ref[:, (LEAF_DEV - REACH) * LEAF :]
    head_ref[:, :wide] = rhs_ref[:, :wide]
    copies[1].wait()
    parts = []
    for t in range(LEAF_DEV):
        block = rhs_ref[:, t * LEAF : (t + 1) * LEAF]
        parts.append(dot(block, basis_ref[t], NT).astype(jnp.bfloat16))
    copies[2].wait()
    root = dot(parts[0], transfer_ref[0])
    for t in range(1, LEAF_DEV):
        root = root + dot(parts[t], transfer_ref[t])
    packed = jnp.concatenate([root[:8], root[8:]], 1)
    for j in range(LINE):
        sends_ref[8 * j : 8 * (j + 1), :] = packed
    coeffs = jnp.concatenate(parts, 1)
    coeffs_ref[...] = coeffs
    tail_ref[:, wide:] = coeffs[:, (LEAF_DEV - REACH) * RANK :]
    head_ref[:, wide:] = coeffs[:, : REACH * RANK]
    for copy in copies[3:]:
        copy.wait()


def near_kernel(
    near_src, coup_src, rhs_ref, coeffs_ref, lower_ref, upper_ref, tiles_ref, coupling_ref,
    near_ref, field_ref, blocks, leaf_coeffs,
):
    own = near_src[0, 0]
    anchor = own - REACH
    none = LEAF_DEV + 2 * REACH
    wide = REACH * LEAF
    for i in range(REACH):
        blocks[i] = lower_ref[:, i * LEAF : (i + 1) * LEAF]
        blocks[REACH + LEAF_DEV + i] = upper_ref[:, i * LEAF : (i + 1) * LEAF]
        leaf_coeffs[i] = lower_ref[:, wide + i * RANK : wide + (i + 1) * RANK]
        leaf_coeffs[REACH + LEAF_DEV + i] = upper_ref[:, wide + i * RANK : wide + (i + 1) * RANK]
    for t in range(LEAF_DEV):
        blocks[REACH + t] = rhs_ref[:, t * LEAF : (t + 1) * LEAF]
        leaf_coeffs[REACH + t] = coeffs_ref[:, t * RANK : (t + 1) * RANK]
    blocks[none] = jnp.zeros((NRHS, LEAF), jnp.bfloat16)
    leaf_coeffs[none] = jnp.zeros((NRHS, RANK), jnp.bfloat16)

    def place(source):
        return jnp.where(source >= 0, jnp.clip(source - anchor, 0, none - 1), none)

    fields = []
    for t in range(LEAF_DEV):
        picked = jnp.concatenate([blocks[place(near_src[t, n])] for n in range(NEAR)], 1)
        near_ref[:, t * LEAF : (t + 1) * LEAF] = dot(picked, tiles_ref[t].reshape(NEAR * LEAF, LEAF))
        taken = jnp.concatenate([leaf_coeffs[place(coup_src[t, a])] for a in range(ADM)], 1)
        fields.append(dot(taken, coupling_ref[t].reshape(ADM * RANK, RANK)))
    field_ref[...] = jnp.concatenate(fields, 1)


def tree_kernel(got_ref, up_ref, coup_ref, own_ref, after_ref, before_ref, *levels):
    place = lax.axis_index("gz")
    wide = got_ref[...].reshape(LINE, 8, 2 * RANK)
    order = [(z - LEADER) % LINE for z in range(LINE)]
    for z in range(LINE):
        levels[0][0, z] = wide[order[z], :, :RANK]
        levels[0][1, z] = wide[order[z], :, RANK:]
    for h in range(1, TOPL + 1):
        count = LINE >> h
        before = levels[h - 1][...].reshape(2, count, 2, 8, RANK)
        pairs = jnp.concatenate([before[:, :, 0], before[:, :, 1]], -1)
        mat = up_ref[h - 1].reshape(2 * RANK, RANK)
        levels[h][...] = dot_split(pairs.reshape(NRHS * count, 2 * RANK), mat).reshape(2, count, 8, RANK)

    def cluster(h, q):
        return levels[h][:, q].reshape(NRHS, RANK)

    zero = jnp.zeros((NRHS, RANK), jnp.float32)
    fields = []
    for h in range(TOPL + 1):
        count = LINE >> h
        q = place >> h
        if h < TOPL:
            lower = cluster(h, jnp.maximum(q - 1, 0)) * (q > 0).astype(jnp.float32)
            upper = cluster(h, jnp.minimum(q + 1, count - 1)) * (q < count - 1).astype(jnp.float32)
        else:
            lower = upper = zero
        last = cluster(h, count - 1) * (q == 0).astype(jnp.float32)
        first = cluster(h, 0) * (q == count - 1).astype(jnp.float32)
        sides = jnp.concatenate(
            [
                jnp.concatenate([lower, upper], 1),
                jnp.concatenate([last, zero], 1),
                jnp.concatenate([zero, first], 1),
            ],
            0,
        )
        fields.append(dot_split(sides, coup_ref[h].reshape(2 * RANK, RANK)))
    incoming = fields[TOPL]
    for h in range(TOPL, 0, -1):
        parity = (place >> (h - 1)) & 1
        incoming = fields[h - 1] + dot_split(incoming, up_ref[h - 1, parity], NT)
    own_ref[...] = incoming[:NRHS]
    after_ref[...] = incoming[NRHS : 2 * NRHS]
    before_ref[...] = incoming[2 * NRHS :]


def out_kernel(own_ref, lower_ref, upper_ref, field_ref, near_ref, transfer_ref, basis_ref, out_ref):
    incoming = own_ref[...] + lower_ref[...] + upper_ref[...]
    spread = dot_split(incoming, transfer_ref[...].reshape(LEAF_DEV * RANK, RANK), NT)
    potential = (field_ref[...] + spread).astype(jnp.bfloat16)
    for t in range(LEAF_DEV):
        far = dot(potential[:, t * RANK : (t + 1) * RANK], basis_ref[t])
        at = slice(t * LEAF, (t + 1) * LEAF)
        out_ref[:, at] = (far + near_ref[:, at]).astype(jnp.bfloat16)


def shifted(values, count, distance):
    route = [(i, i + distance) for i in range(count) if 0 <= i + distance < count]
    return lax.ppermute(values, AXES, route)


def call(kernel, outs, scratch=(), ins=(), flops=0, moved=0, name=None):
    return pl.pallas_call(
        kernel,
        out_shape=[jax.ShapeDtypeStruct(shape, dtype) for shape, dtype in outs],
        in_specs=list(ins),
        out_specs=[VMEM] * len(outs),
        scratch_shapes=list(scratch),
        cost_estimate=pl.CostEstimate(flops=flops, bytes_accessed=moved, transcendentals=0),
        compiler_params=pltpu.CompilerParams(vmem_limit_bytes=24 * 2**20),
        name=name,
    )


def local(
    rhs,
    leaf_basis,
    leaf_transfer,
    leaf_coupling,
    coupling_sources,
    near_tiles,
    near_sources,
    top_transfer,
    cluster_coupling,
):
    bf16, f32 = jnp.bfloat16, jnp.float32
    count = lax.axis_size(AXES)
    width = LEAF_DEV * LEAF
    ranks = LEAF_DEV * RANK
    inputs = (
        rhs, leaf_basis, leaf_transfer, top_transfer, cluster_coupling,
        near_sources, coupling_sources, leaf_coupling, near_tiles,
    )
    inputs = [pltpu.with_memory_space_constraint(x, pltpu.HBM) for x in inputs]
    coeffs, sends, tail, head, *kept = call(
        coeff_kernel,
        [
            ((NRHS, ranks), bf16),
            ((LINE * 8, 2 * RANK), f32),
            ((NRHS, EDGE), bf16),
            ((NRHS, EDGE), bf16),
        ]
        + [(x.shape, x.dtype) for x in inputs],
        scratch=[pltpu.SemaphoreType.DMA((STAGED,))],
        ins=[HBM] * STAGED,
        flops=2 * NRHS * ranks * (LEAF + RANK),
        moved=2**21,
        name="coeffs",
    )(*inputs)
    rhs, leaf_basis, leaf_transfer, top_transfer, cluster_coupling = kept[:5]
    near_sources, coupling_sources, leaf_coupling, near_tiles = kept[5:]
    ring = [(LEADER + i) % LINE for i in range(LINE)]
    got = lax.all_to_all(sends, "gz", 0, 0, tiled=True, axis_index_groups=[ring])
    lower = shifted(tail, count, 1)
    upper = shifted(head, count, -1)
    near, field = call(
        near_kernel,
        [((NRHS, width), f32), ((NRHS, ranks), f32)],
        scratch=[
            pltpu.VMEM((LEAF_DEV + 2 * REACH + 1, NRHS, LEAF), bf16),
            pltpu.VMEM((LEAF_DEV + 2 * REACH + 1, NRHS, RANK), bf16),
        ],
        ins=[SMEM, SMEM] + [VMEM] * 6,
        flops=2 * NRHS * LEAF_DEV * (NEAR * LEAF * LEAF + ADM * RANK * RANK),
        moved=2**21,
        name="near",
    )(near_sources, coupling_sources, rhs, coeffs, lower, upper, near_tiles, leaf_coupling)
    own, after, before = call(
        tree_kernel,
        [((NRHS, RANK), f32)] * 3,
        scratch=[pltpu.VMEM((2, LINE >> h, 8, RANK), f32) for h in range(TOPL + 1)],
        ins=[VMEM] * 3,
        flops=2**23,
        moved=2**18,
        name="tree",
    )(got, top_transfer, cluster_coupling)
    from_lower = shifted(after, count, LINE)
    from_upper = shifted(before, count, -LINE)
    return call(
        out_kernel,
        [((NRHS, width), bf16)],
        ins=[VMEM] * 7,
        flops=2 * NRHS * ranks * (LEAF + RANK),
        moved=2**18,
        name="out",
    )(own, from_lower, from_upper, field, near, leaf_transfer, leaf_basis)[0]


def solution(mesh):
    placed = (
        P(None, AXES),
        P(AXES, None, None),
        P(AXES, None, None),
        P(AXES, None, None, None),
        P(AXES, None),
        P(AXES, None, None, None),
        P(AXES, None),
        P(),
        P(),
    )
    return jax.shard_map(
        local, mesh=mesh, in_specs=placed, out_specs=P(None, AXES), check_vma=False
    )
```

time: 148 us -> 41.8 us (0.28)
  the two profiles are of different devices: /device:TPU:6 before, /device:TPU:25 now
where the time goes in v1:
time: 41.8 us; the launch traced here: 41.5 us
  starting transfers between devices  31.2 us (75%)
  Pallas kernels  6.21 us (15%)
  waiting for transfers between devices  4.03 us (10%)
    all_to_all x1, starting transfers between devices, local(): lax.all_to_all(sends, 'gz', 0, 0, tiled=True, axis_index_groups=[ring])  15.6 us
    ppermute x4, starting transfers between devices, shifted(): return lax.ppermute(values, AXES, route)  15.6 us
    ppermute x4, waiting for transfers between devices, shifted(): return lax.ppermute(values, AXES, route)  4.03 us
    pallas_call x1, Pallas kernels, local(): call(coeff_kernel, [((NRHS, ranks), bf16), ((LINE * 8, 2 * RANK), f32), (...  2.54 us
    pallas_call x1, Pallas kernels, local(): call(tree_kernel, [((NRHS, RANK), f32)] * 3, scratch=[pltpu.VMEM((2, LINE...  1.58 us
    pallas_call x1, Pallas kernels, local(): call(near_kernel, [((NRHS, width), f32), ((NRHS, ranks), f32)], scratch=[...  1.11 us
    pallas_call x1, Pallas kernels, local(): call(out_kernel, [((NRHS, width), bf16)], ins=[VMEM] * 7, flops=2 * NRHS...  0.98 us
  transfers between devices with their start and end apart: 5, of which 1 were waited for; matrix products, arithmetic and copies ran while one was open for 0% of the time, Pallas kernels for 6%

profile of v1, /device:TPU:25, one launch (start us, length us, event | category | flops | bytes accessed | tf_op | source)
XLA Modules:
  0.0 41.5 jit_solution(13933334994134462971)
XLA Ops:
  0.0 2.5 %coeffs.1 = (bf16[16,256]{1,0:T(8,128)(2,1)S(1)}, f32[128,128]{1,0:T(8,128)}, bf16[16,640]{1,0:T(8,128)(2,1)S(1)}, bf16[16,640]{1,0:T(8,128)(2,1)S(1)}, bf16[16,...) custom-call(bf16[16,1024]{1,0:T(8,128)(2,1)} %refs_0_.1, ...), custom_call_target="tpu_custom_call" | custom-call | flops 2621440 | bytes 2097152 | tf_op jit(solution)/shard_map/coeffs/pallas_call | solution.py:198
  2.6 15.6 %all-to-all-start = ((f32[16,8,128]{2,1,0:T(8,128)}), f32[16,8,128]{2,1,0:T(8,128)S(1)}, u32[]{:S(2)}, u32[]{:S(2)}) async-start(f32[16,8,128]{2,1,0:T(8,128)} %bitcast), calls=%async_computation | async-start | bytes 131072 | tf_op jit(solution)/shard_map/all_to_all | solution.py:216
  18.2 3.1 %collective-permute-start.2 = (bf16[16,640]{1,0:T(8,128)(2,1)S(1)}, bf16[16,640]{1,0:T(8,128)(2,1)S(1)}, u32[]{:S(2)}, u32[]{:S(2)}) collective-permute-start(bf16[16,640]{1,0:T(8,128)(2,1)S(1)} %get-tuple-element.33), channel_id=1, source_target_pairs={{0,1},{1,2},{2,3},{3,4},{4,5},{5,6},{6,7},{7,8},{8,9},{9,10},{10,1... | collective-permute-start | bytes 61448 | tf_op jit(solution)/shard_map/ppermute | solution.py:162
  21.2 4.3 %collective-permute-start.3 = (bf16[16,640]{1,0:T(8,128)(2,1)S(1)}, bf16[16,640]{1,0:T(8,128)(2,1)S(1)}, u32[]{:S(2)}, u32[]{:S(2)}) collective-permute-start(bf16[16,640]{1,0:T(8,128)(2,1)S(1)} %get-tuple-element.34), channel_id=1, source_target_pairs={{1,0},{2,1},{3,2},{4,3},{5,4},{6,5},{7,6},{8,7},{9,8},{10,9},{11,1... | collective-permute-start | bytes 61448 | tf_op jit(solution)/shard_map/ppermute | solution.py:162
  25.6 0.0 all-to-all-done
  25.6 1.6 %tree.1 = (f32[16,64]{1,0:T(8,128)S(1)}, f32[16,64]{1,0:T(8,128)S(1)}, f32[16,64]{1,0:T(8,128)S(1)}) custom-call(f32[128,128]{1,0:T(8,128)S(1)} %bitcast.2, bf16[4,2,64,64]{3,2,1,0:T(8,128)(2,1)S(1)} %get-tuple-element.24.up_ref, bf16[5,2,64,64]{3,2,1,0:T(8,128)(2,1)S(1)} %get-tuple-element.25.coup_ref), custom_call_target="tpu_custom_call" | custom-call | flops 8388608 | bytes 262144 | tf_op jit(solution)/shard_map/tree/pallas_call | solution.py:231
  27.2 6.3 %collective-permute-start = (f32[16,64]{1,0:T(8,128)S(1)}, f32[16,64]{1,0:T(8,128)S(1)}, u32[]{:S(2)}, u32[]{:S(2)}) collective-permute-start(f32[16,64]{1,0:T(8,128)S(1)} %get-tuple-element.27), channel_id=1, source_target_pairs={{0,16},{1,17},{2,18},{3,19},{4,20},{5,21},{6,22},{7,23},{8,24},{9,... | collective-permute-start | bytes 12296 | tf_op jit(solution)/shard_map/ppermute | solution.py:162
  33.4 1.9 %collective-permute-start.1 = (f32[16,64]{1,0:T(8,128)S(1)}, f32[16,64]{1,0:T(8,128)S(1)}, u32[]{:S(2)}, u32[]{:S(2)}) collective-permute-start(f32[16,64]{1,0:T(8,128)S(1)} %get-tuple-element.28), channel_id=1, source_target_pairs={{16,0},{17,1},{18,2},{19,3},{20,4},{21,5},{22,6},{23,7},{24,8},{25... | collective-permute-start | bytes 12296 | tf_op jit(solution)/shard_map/ppermute | solution.py:162
  35.4 0.0 collective-permute-done.2.lower_ref
  35.4 0.0 collective-permute-done.3.upper_ref
  35.4 1.1 %near.1 = (f32[16,1024]{1,0:T(8,128)S(1)}, f32[16,256]{1,0:T(8,128)S(1)}) custom-call(s32[4,3]{1,0:T(4,128)S(1)} %get-tuple-element.29.near_src, s32[4,6]{1,0:T(4,128)S(1)} %get-tuple-element.30.coup_src, bf16[16,1024]{1,0:T(8,128)(2,1)S(1)} %get-tuple-element.31.rhs_ref, bf16[16,256]{1,0:T(8,128)(2,1)S(1)} %get-tuple-element.32.coeffs_ref, ...), custom_call_target="tpu_custom_call" | custom-call | flops 28311552 | bytes 2097152 | tf_op jit(solution)/shard_map/near/pallas_call | solution.py:219
  36.5 0.0 collective-permute-done.lower_ref
  36.5 4.0 %collective-permute-done.1.upper_ref = f32[16,64]{1,0:T(8,128)S(1)} collective-permute-done((f32[16,64]{1,0:T(8,128)S(1)}, f32[16,64]{1,0:T(8,128)S(1)}, u32[]{:S(2)}, u32[]{:S(2)}) %collective-permute-start.1) | collective-permute-done | bytes 4128 | tf_op jit(solution)/shard_map/ppermute | solution.py:162
  40.5 1.0 %out.1 = bf16[16,1024]{1,0:T(8,128)(2,1)} custom-call(f32[16,64]{1,0:T(8,128)S(1)} %get-tuple-element.26.own_ref, f32[16,64]{1,0:T(8,128)S(1)} %collective-permute-done.lower_ref, f32[16,64]{1,0:T(8,128)S(1)} %collective-permute-done.1.upper_ref, f32[16,256]{1,0:T(8,128)S(1)} %get-tuple-element.37.field_ref, f32[16,1024]{1,0:T(8,128)S(1)} %get-tuple-element.38.near_ref, ...), custom_call_target="tpu_custom_call" | custom-call | flops 2621440 | bytes 262144 | tf_op jit(solution)/shard_map/out/pallas_call | solution.py:242
Async XLA Ops:
  2.6 23.0 %all-to-all-start = ((f32[16,8,128]{2,1,0:T(8,128)}), f32[16,8,128]{2,1,0:T(8,128)S(1)}, u32[]{:S(2)}, u32[]{:S(2)}) async-start(f32[16,8,128]{2,1,0:T(8,128)} %bitcast), calls=%async_computation | async-start | bytes 131072 | tf_op jit(solution)/shard_map/all_to_all | solution.py:216
  18.2 17.2 %collective-permute-start.2 = (bf16[16,640]{1,0:T(8,128)(2,1)S(1)}, bf16[16,640]{1,0:T(8,128)(2,1)S(1)}, u32[]{:S(2)}, u32[]{:S(2)}) collective-permute-start(bf16[16,640]{1,0:T(8,128)(2,1)S(1)} %get-tuple-element.33), channel_id=1, source_target_pairs={{0,1},{1,2},{2,3},{3,4},{4,5},{5,6},{6,7},{7,8},{8,9},{9,10},{10,1... | collective-permute-start | bytes 61448 | tf_op jit(solution)/shard_map/ppermute | solution.py:162
  21.2 14.1 %collective-permute-start.3 = (bf16[16,640]{1,0:T(8,128)(2,1)S(1)}, bf16[16,640]{1,0:T(8,128)(2,1)S(1)}, u32[]{:S(2)}, u32[]{:S(2)}) collective-permute-start(bf16[16,640]{1,0:T(8,128)(2,1)S(1)} %get-tuple-element.34), channel_id=1, source_target_pairs={{1,0},{2,1},{3,2},{4,3},{5,4},{6,5},{7,6},{8,7},{9,8},{10,9},{11,1... | collective-permute-start | bytes 61448 | tf_op jit(solution)/shard_map/ppermute | solution.py:162
  27.2 9.4 %collective-permute-start = (f32[16,64]{1,0:T(8,128)S(1)}, f32[16,64]{1,0:T(8,128)S(1)}, u32[]{:S(2)}, u32[]{:S(2)}) collective-permute-start(f32[16,64]{1,0:T(8,128)S(1)} %get-tuple-element.27), channel_id=1, source_target_pairs={{0,16},{1,17},{2,18},{3,19},{4,20},{5,21},{6,22},{7,23},{8,24},{9,... | collective-permute-start | bytes 12296 | tf_op jit(solution)/shard_map/ppermute | solution.py:162
  33.4 7.1 %collective-permute-start.1 = (f32[16,64]{1,0:T(8,128)S(1)}, f32[16,64]{1,0:T(8,128)S(1)}, u32[]{:S(2)}, u32[]{:S(2)}) collective-permute-start(f32[16,64]{1,0:T(8,128)S(1)} %get-tuple-element.28), channel_id=1, source_target_pairs={{16,0},{17,1},{18,2},{19,3},{20,4},{21,5},{22,6},{23,7},{24,8},{25... | collective-permute-start | bytes 12296 | tf_op jit(solution)/shard_map/ppermute | solution.py:162

commit v2 on v1

v2 whole, which is shorter than its diff:
```python
import jax
import jax.numpy as jnp
from jax import lax
from jax.experimental import pallas as pl
from jax.experimental.pallas import tpu as pltpu
from jax.sharding import PartitionSpec as P

LEAF = 256
RANK = 64
NRHS = 16
NEAR = 3
ADM = 6
TOPL = 4
LEAF_DEV = 4
REACH = 2
LINE = 16
PAIR = 2 * LINE
LEADER = 11
MEMBERS = [(1, LEADER), (0, LEADER)] + [(line, z) for z in [12, 10, 9, 8, 7, 6, 5, 4, 3, 2, 1, 0, 15, 14, 13] for line in range(2)]
AXES = ("gx", "gy", "gz")
EDGE = REACH * (LEAF + RANK)
VMEM = pl.BlockSpec(memory_space=pltpu.VMEM)
SMEM = pl.BlockSpec(memory_space=pltpu.SMEM)
HBM = pl.BlockSpec(memory_space=pltpu.HBM)
STAGED = 7
HELD = 2
EARLY = 6
NT = (((1,), (1,)), ((), ()))
NN = (((1,), (0,)), ((), ()))


def dot(a, b, dims=NN):
    return lax.dot_general(a, b, dims, preferred_element_type=jnp.float32)


def dot_split(a, b, dims=NN):
    high = a.astype(jnp.bfloat16)
    low = (a - high.astype(jnp.float32)).astype(jnp.bfloat16)
    both = dot(jnp.concatenate([high, low], 0), b, dims)
    return both[: a.shape[0]] + both[a.shape[0] :]


def hold(staged, kept, done):
    return [pltpu.make_async_copy(staged[i], kept[i], done.at[i]) for i in range(HELD)]


def coeff_kernel(*refs):
    count = STAGED + HELD
    staged, coeffs_ref, sends_ref, head_ref, tail_ref = refs[:count], *refs[count : count + 4]
    kept, done, held = refs[count + 4 : -2], refs[-2], refs[-1]
    copies = [
        pltpu.make_async_copy(staged[i], kept[i], done.at[i]) for i in range(STAGED)
    ]
    for copy in copies:
        copy.start()
    early = lax.axis_index("gz") < EARLY

    @pl.when(early)
    def _():
        for copy in hold(staged[STAGED:], kept[STAGED:], held):
            copy.start()

    rhs_ref, basis_ref, transfer_ref = kept[:3]
    copies[0].wait()
    wide = REACH * LEAF
    tail_ref[:, :wide] = rhs_ref[:, (LEAF_DEV - REACH) * LEAF :]
    head_ref[:, :wide] = rhs_ref[:, :wide]
    copies[1].wait()
    parts = []
    for t in range(LEAF_DEV):
        block = rhs_ref[:, t * LEAF : (t + 1) * LEAF]
        parts.append(dot(block, basis_ref[t], NT).astype(jnp.bfloat16))
    copies[2].wait()
    root = dot(parts[0], transfer_ref[0])
    for t in range(1, LEAF_DEV):
        root = root + dot(parts[t], transfer_ref[t])
    packed = jnp.concatenate([root[:8], root[8:]], 1)
    packed = jnp.concatenate([packed, packed], 0).astype(jnp.bfloat16)
    for j in range(PAIR // 2):
        sends_ref[16 * j : 16 * (j + 1), :] = packed
    coeffs = jnp.concatenate(parts, 1)
    coeffs_ref[...] = coeffs
    tail_ref[:, wide:] = coeffs[:, (LEAF_DEV - REACH) * RANK :]
    head_ref[:, wide:] = coeffs[:, : REACH * RANK]
    for copy in copies[3:]:
        copy.wait()

    @pl.when(early)
    def _():
        for copy in hold(staged[STAGED:], kept[STAGED:], held):
            copy.wait()


def near_kernel(
    near_src, coup_src, rhs_ref, coeffs_ref, upper_ref, lower_ref, coupling_hbm, tiles_hbm,
    coupling_in, tiles_in, near_ref, field_ref, coupling_ref, tiles_ref, blocks, leaf_coeffs, held,
):
    late = lax.axis_index("gz") >= EARLY

    @pl.when(late)
    def _():
        for copy in hold([coupling_hbm, tiles_hbm], [coupling_ref, tiles_ref], held):
            copy.start()

    own = near_src[0, 0]
    anchor = own - REACH
    none = LEAF_DEV + 2 * REACH
    wide = REACH * LEAF
    for i in range(REACH):
        blocks[i] = lower_ref[:, i * LEAF : (i + 1) * LEAF]
        blocks[REACH + LEAF_DEV + i] = upper_ref[:, i * LEAF : (i + 1) * LEAF]
        leaf_coeffs[i] = lower_ref[:, wide + i * RANK : wide + (i + 1) * RANK]
        leaf_coeffs[REACH + LEAF_DEV + i] = upper_ref[:, wide + i * RANK : wide + (i + 1) * RANK]
    for t in range(LEAF_DEV):
        blocks[REACH + t] = rhs_ref[:, t * LEAF : (t + 1) * LEAF]
        leaf_coeffs[REACH + t] = coeffs_ref[:, t * RANK : (t + 1) * RANK]
    blocks[none] = jnp.zeros((NRHS, LEAF), jnp.bfloat16)
    leaf_coeffs[none] = jnp.zeros((NRHS, RANK), jnp.bfloat16)

    def place(source):
        return jnp.where(source >= 0, jnp.clip(source - anchor, 0, none - 1), none)

    @pl.when(late)
    def _():
        for copy in hold([coupling_hbm, tiles_hbm], [coupling_ref, tiles_ref], held):
            copy.wait()

    fields = []
    for t in range(LEAF_DEV):
        picked = jnp.concatenate([blocks[place(near_src[t, n])] for n in range(NEAR)], 1)
        near_ref[:, t * LEAF : (t + 1) * LEAF] = dot(picked, tiles_ref[t].reshape(NEAR * LEAF, LEAF))
        taken = jnp.concatenate([leaf_coeffs[place(coup_src[t, a])] for a in range(ADM)], 1)
        fields.append(dot(taken, coupling_ref[t].reshape(ADM * RANK, RANK)))
    field_ref[...] = jnp.concatenate(fields, 1)


def tree_kernel(got_ref, up_ref, coup_ref, own_ref, cross_ref, *levels):
    spot = lax.axis_index("gz")
    half = lax.axis_index("gy") & 1
    place = half * LINE + spot
    wide = got_ref[...].astype(jnp.float32).reshape(PAIR, 8, 2 * RANK)
    for j, (line, z) in enumerate(MEMBERS):
        levels[0][0, line * LINE + z] = wide[j, :, :RANK]
        levels[0][1, line * LINE + z] = wide[j, :, RANK:]
    for h in range(1, TOPL + 1):
        count = PAIR >> h
        before = levels[h - 1][...].reshape(2, count, 2, 8, RANK)
        pairs = jnp.concatenate([before[:, :, 0], before[:, :, 1]], -1)
        mat = up_ref[h - 1].reshape(2 * RANK, RANK)
        levels[h][...] = dot_split(pairs.reshape(NRHS * count, 2 * RANK), mat).reshape(2, count, 8, RANK)

    def cluster(h, q, used):
        return levels[h][:, q].reshape(NRHS, RANK) * used.astype(jnp.float32)

    fields = []
    for h in range(TOPL + 1):
        count = PAIR >> h
        q = place >> h
        low = spot >> h
        sides = [
            cluster(h, jnp.maximum(q - 1, 0), q > 0),
            cluster(h, jnp.minimum(q + 1, count - 1), q < count - 1),
            cluster(h, count - 1, (half == 1) & (low == 0)),
            cluster(h, 0, (half == 0) & (low == (LINE >> h) - 1)),
        ]
        rows = jnp.concatenate([jnp.concatenate(sides[:2], 1), jnp.concatenate(sides[2:], 1)], 0)
        fields.append(dot_split(rows, coup_ref[h].reshape(2 * RANK, RANK)))
    incoming = fields[TOPL]
    for h in range(TOPL, 0, -1):
        parity = (spot >> (h - 1)) & 1
        incoming = fields[h - 1] + dot_split(incoming, up_ref[h - 1, parity], NT)
    own_ref[...] = incoming[:NRHS]
    cross_ref[...] = incoming[NRHS:]


def out_kernel(own_ref, cross_ref, field_ref, near_ref, transfer_ref, basis_ref, out_ref):
    incoming = own_ref[...] + cross_ref[...]
    spread = dot_split(incoming, transfer_ref[...].reshape(LEAF_DEV * RANK, RANK), NT)
    potential = (field_ref[...] + spread).astype(jnp.bfloat16)
    for t in range(LEAF_DEV):
        far = dot(potential[:, t * RANK : (t + 1) * RANK], basis_ref[t])
        at = slice(t * LEAF, (t + 1) * LEAF)
        out_ref[:, at] = (far + near_ref[:, at]).astype(jnp.bfloat16)


def crossed(values, count):
    route = []
    for line in range(1, count // LINE - 1, 2):
        for z in range(LINE):
            low = line * LINE + z
            route += [(low, low + LINE), (low + LINE, low)]
    return lax.ppermute(values, AXES, route)


def shifted(values, count, distance):
    route = [(i, i + distance) for i in range(count) if 0 <= i + distance < count]
    return lax.ppermute(values, AXES, route)


def call(kernel, outs, scratch=(), ins=(), flops=0, moved=0, name=None, aliases=None):
    return pl.pallas_call(
        kernel,
        out_shape=[jax.ShapeDtypeStruct(shape, dtype) for shape, dtype in outs],
        in_specs=list(ins),
        out_specs=[VMEM] * len(outs),
        scratch_shapes=list(scratch),
        cost_estimate=pl.CostEstimate(flops=flops, bytes_accessed=moved, transcendentals=0),
        compiler_params=pltpu.CompilerParams(vmem_limit_bytes=24 * 2**20),
        input_output_aliases=aliases or {},
        name=name,
    )


def local(
    rhs,
    leaf_basis,
    leaf_transfer,
    leaf_coupling,
    coupling_sources,
    near_tiles,
    near_sources,
    top_transfer,
    cluster_coupling,
):
    bf16, f32 = jnp.bfloat16, jnp.float32
    count = lax.axis_size(AXES)
    width = LEAF_DEV * LEAF
    ranks = LEAF_DEV * RANK
    inputs = (
        rhs, leaf_basis, leaf_transfer, top_transfer, cluster_coupling,
        near_sources, coupling_sources, leaf_coupling, near_tiles,
    )
    inputs = [pltpu.with_memory_space_constraint(x, pltpu.HBM) for x in inputs]
    coeffs, sends, head, tail, *kept = call(
        coeff_kernel,
        [
            ((NRHS, ranks), bf16),
            ((PAIR * 8, 2 * RANK), bf16),
            ((NRHS, EDGE), bf16),
            ((NRHS, EDGE), bf16),
        ]
        + [(x.shape, x.dtype) for x in inputs],
        scratch=[pltpu.SemaphoreType.DMA((STAGED,)), pltpu.SemaphoreType.DMA((HELD,))],
        ins=[HBM] * (STAGED + HELD),
        flops=2 * NRHS * ranks * (LEAF + RANK),
        moved=2**21,
        name="coeffs",
    )(*inputs)
    rhs, leaf_basis, leaf_transfer, top_transfer, cluster_coupling = kept[:5]
    near_sources, coupling_sources, coupling_kept, tiles_kept = kept[5:]
    pairs = [
        [(2 * k + line) * LINE + z for line, z in MEMBERS]
        for k in range(lax.axis_size("gy") // 2)
    ]
    got = lax.all_to_all(sends, ("gy", "gz"), 0, 0, tiled=True, axis_index_groups=pairs)
    upper = shifted(head, count, -1)
    lower = shifted(tail, count, 1)
    near, field, _, _ = call(
        near_kernel,
        [((NRHS, width), f32), ((NRHS, ranks), f32)]
        + [(x.shape, x.dtype) for x in (coupling_kept, tiles_kept)],
        scratch=[
            pltpu.VMEM((LEAF_DEV + 2 * REACH + 1, NRHS, LEAF), bf16),
            pltpu.VMEM((LEAF_DEV + 2 * REACH + 1, NRHS, RANK), bf16),
            pltpu.SemaphoreType.DMA((HELD,)),
        ],
        ins=[SMEM, SMEM] + [VMEM] * 4 + [HBM] * 2 + [VMEM] * 2,
        aliases={8: 2, 9: 3},
        flops=2 * NRHS * LEAF_DEV * (NEAR * LEAF * LEAF + ADM * RANK * RANK),
        moved=2**21,
        name="near",
    )(near_sources, coupling_sources, rhs, coeffs, upper, lower, *inputs[-HELD:], coupling_kept, tiles_kept)
    own, cross = call(
        tree_kernel,
        [((NRHS, RANK), f32)] * 2,
        scratch=[pltpu.VMEM((2, PAIR >> h, 8, RANK), f32) for h in range(TOPL + 1)],
        ins=[VMEM] * 3,
        flops=2**23,
        moved=2**18,
        name="tree",
    )(got, top_transfer, cluster_coupling)
    cross = crossed(cross, count)
    return call(
        out_kernel,
        [((NRHS, width), bf16)],
        ins=[VMEM] * 6,
        flops=2 * NRHS * ranks * (LEAF + RANK),
        moved=2**18,
        name="out",
    )(own, cross, field, near, leaf_transfer, leaf_basis)[0]


def solution(mesh):
    placed = (
        P(None, AXES),
        P(AXES, None, None),
        P(AXES, None, None),
        P(AXES, None, None, None),
        P(AXES, None),
        P(AXES, None, None, None),
        P(AXES, None),
        P(),
        P(),
    )
    return jax.shard_map(
        local, mesh=mesh, in_specs=placed, out_specs=P(None, AXES), check_vma=False
    )
```

time: 41.8 us -> 35.8 us (0.86)
  the two profiles are of different devices: /device:TPU:25 before, /device:TPU:6 now
where the time goes in v2:
time: 35.8 us; the launch traced here: 35.4 us
  starting transfers between devices  26.1 us (73%)
  Pallas kernels  6.24 us (17%)
  waiting for transfers between devices  2.94 us (8%)
    all_to_all x1, starting transfers between devices, local(): lax.all_to_all(sends, ('gy', 'gz'), 0, 0, tiled=True, axis_index_groups=p...  16.8 us
    ppermute x2, starting transfers between devices, shifted(): return lax.ppermute(values, AXES, route)  5.84 us
    ppermute x1, starting transfers between devices, crossed(): return lax.ppermute(values, AXES, route)  3.42 us
    pallas_call x1, Pallas kernels, local(): call(coeff_kernel, [((NRHS, ranks), bf16), ((PAIR * 8, 2 * RANK), bf16),...  2.53 us
    pallas_call x1, Pallas kernels, local(): call(tree_kernel, [((NRHS, RANK), f32)] * 2, scratch=[pltpu.VMEM((2, PAIR...  1.58 us
    ppermute x2, waiting for transfers between devices, shifted(): return lax.ppermute(values, AXES, route)  1.27 us
    ppermute x1, waiting for transfers between devices, crossed(): return lax.ppermute(values, AXES, route)  1.25 us
    pallas_call x1, Pallas kernels, local(): call(near_kernel, [((NRHS, width), f32), ((NRHS, ranks), f32)] + [(x.shap...  1.14 us
  transfers between devices with their start and end apart: 4, of which 3 were waited for; matrix products, arithmetic and copies ran while one was open for 0% of the time, Pallas kernels for 8%

profile of v2, /device:TPU:6, one launch (start us, length us, event | category | flops | bytes accessed | tf_op | source)
XLA Modules:
  0.0 35.4 jit_solution(14502981471088294086)
XLA Ops:
  0.0 2.5 %coeffs.1 = (bf16[16,256]{1,0:T(8,128)(2,1)S(1)}, bf16[256,128]{1,0:T(8,128)(2,1)}, bf16[16,640]{1,0:T(8,128)(2,1)S(1)}, bf16[16,640]{1,0:T(8,128)(2,1)S(1)}, bf...) custom-call(bf16[16,1024]{1,0:T(8,128)(2,1)} %refs_0_.1, ...), custom_call_target="tpu_custom_call" | custom-call | flops 2621440 | bytes 2097152 | tf_op jit(solution)/shard_map/coeffs/pallas_call | solution.py:234
  2.5 16.8 %all-to-all-start = ((bf16[32,8,128]{2,1,0:T(8,128)(2,1)}), bf16[32,8,128]{2,1,0:T(8,128)(2,1)S(1)}, u32[]{:S(2)}, u32[]{:S(2)}) async-start(bf16[32,8,128]{2,1,0:T(8,128)(2,1)} %bitcast), calls=%async_computation | async-start | bytes 131072 | tf_op jit(solution)/shard_map/all_to_all | solution.py:255
  19.4 3.3 %collective-permute-start.1 = (bf16[16,640]{1,0:T(8,128)(2,1)S(1)}, bf16[16,640]{1,0:T(8,128)(2,1)S(1)}, u32[]{:S(2)}, u32[]{:S(2)}) collective-permute-start(bf16[16,640]{1,0:T(8,128)(2,1)S(1)} %get-tuple-element.31), channel_id=1, source_target_pairs={{1,0},{2,1},{3,2},{4,3},{5,4},{6,5},{7,6},{8,7},{9,8},{10,9},{11,1... | collective-permute-start | bytes 61448 | tf_op jit(solution)/shard_map/ppermute | solution.py:197
  22.7 2.6 %collective-permute-start.2 = (bf16[16,640]{1,0:T(8,128)(2,1)S(1)}, bf16[16,640]{1,0:T(8,128)(2,1)S(1)}, u32[]{:S(2)}, u32[]{:S(2)}) collective-permute-start(bf16[16,640]{1,0:T(8,128)(2,1)S(1)} %get-tuple-element.32), channel_id=1, source_target_pairs={{0,1},{1,2},{2,3},{3,4},{4,5},{5,6},{6,7},{7,8},{8,9},{9,10},{10,1... | collective-permute-start | bytes 61448 | tf_op jit(solution)/shard_map/ppermute | solution.py:197
  25.3 0.4 %all-to-all-done = bf16[32,8,128]{2,1,0:T(8,128)(2,1)S(1)} async-done(((bf16[32,8,128]{2,1,0:T(8,128)(2,1)}), bf16[32,8,128]{2,1,0:T(8,128)(2,1)S(1)}, u32[]{:S(2)}, u32[]{:S(2)}) %all-to-all-start) | async-done | bytes 65568 | tf_op jit(solution)/shard_map/all_to_all | solution.py:255
  25.7 1.6 %tree.1 = (f32[16,64]{1,0:T(8,128)S(1)}, f32[16,64]{1,0:T(8,128)S(1)}) custom-call(bf16[256,128]{1,0:T(8,128)(2,1)S(1)} %bitcast.2, bf16[4,2,64,64]{3,2,1,0:T(8,128)(2,1)S(1)} %get-tuple-element.23.up_ref, bf16[5,2,64,64]{3,2,1,0:T(8,128)(2,1)S(1)} %get-tuple-element.24.coup_ref), custom_call_target="tpu_custom_call" | custom-call | flops 8388608 | bytes 262144 | tf_op jit(solution)/shard_map/tree/pallas_call | solution.py:273
  27.3 3.4 %collective-permute-start = (f32[16,64]{1,0:T(8,128)S(1)}, f32[16,64]{1,0:T(8,128)S(1)}, u32[]{:S(2)}, u32[]{:S(2)}) collective-permute-start(f32[16,64]{1,0:T(8,128)S(1)} %get-tuple-element.26), channel_id=1, source_target_pairs={{16,32},{32,16},{17,33},{33,17},{18,34},{34,18},{19,35},{35,19},{2... | collective-permute-start | bytes 12296 | tf_op jit(solution)/shard_map/ppermute | solution.py:192
  30.7 0.0 collective-permute-done.1.upper_ref
  30.7 1.3 %collective-permute-done.2.lower_ref = bf16[16,640]{1,0:T(8,128)(2,1)S(1)} collective-permute-done((bf16[16,640]{1,0:T(8,128)(2,1)S(1)}, bf16[16,640]{1,0:T(8,128)(2,1)S(1)}, u32[]{:S(2)}, u32[]{:S(2)}) %collective-permute-start.2) | collective-permute-done | bytes 20512 | tf_op jit(solution)/shard_map/ppermute | solution.py:197
  32.0 1.1 %near.1 = (f32[16,1024]{1,0:T(8,128)S(1)}, f32[16,256]{1,0:T(8,128)S(1)}, bf16[4,6,64,64]{3,2,1,0:T(8,128)(2,1)S(1)}, bf16[4,3,256,256]{3,2,1,0:T(8,128)(2,1)S(1)}) custom-call(s32[4,3]{1,0:T(4,128)S(1)} %get-tuple-element.27.near_src, s32[4,6]{1,0:T(4,128)S(1)} %get-tuple-element.28.coup_src, ...), custom_call_target="tpu_custom_call", output_to_operand_aliasing={{2}: (8, {}), {3}: (9, {})} | custom-call | flops 28311552 | bytes 2097152 | tf_op jit(solution)/shard_map/near/pallas_call | solution.py:258
  33.1 1.2 %collective-permute-done.cross_ref = f32[16,64]{1,0:T(8,128)S(1)} collective-permute-done((f32[16,64]{1,0:T(8,128)S(1)}, f32[16,64]{1,0:T(8,128)S(1)}, u32[]{:S(2)}, u32[]{:S(2)}) %collective-permute-start) | collective-permute-done | bytes 4128 | tf_op jit(solution)/shard_map/ppermute | solution.py:192
  34.4 1.0 %out.1 = bf16[16,1024]{1,0:T(8,128)(2,1)} custom-call(f32[16,64]{1,0:T(8,128)S(1)} %get-tuple-element.25.own_ref, f32[16,64]{1,0:T(8,128)S(1)} %collective-permute-done.cross_ref, f32[16,256]{1,0:T(8,128)S(1)} %get-tuple-element.35.field_ref, f32[16,1024]{1,0:T(8,128)S(1)} %get-tuple-element.36.near_ref, ...), custom_call_target="tpu_custom_call" | custom-call | flops 2621440 | bytes 262144 | tf_op jit(solution)/shard_map/out/pallas_call | solution.py:283
Async XLA Ops:
  2.5 23.1 %all-to-all-start = ((bf16[32,8,128]{2,1,0:T(8,128)(2,1)}), bf16[32,8,128]{2,1,0:T(8,128)(2,1)S(1)}, u32[]{:S(2)}, u32[]{:S(2)}) async-start(bf16[32,8,128]{2,1,0:T(8,128)(2,1)} %bitcast), calls=%async_computation | async-start | bytes 131072 | tf_op jit(solution)/shard_map/all_to_all | solution.py:255
  19.4 11.3 %collective-permute-start.1 = (bf16[16,640]{1,0:T(8,128)(2,1)S(1)}, bf16[16,640]{1,0:T(8,128)(2,1)S(1)}, u32[]{:S(2)}, u32[]{:S(2)}) collective-permute-start(bf16[16,640]{1,0:T(8,128)(2,1)S(1)} %get-tuple-element.31), channel_id=1, source_target_pairs={{1,0},{2,1},{3,2},{4,3},{5,4},{6,5},{7,6},{8,7},{9,8},{10,9},{11,1... | collective-permute-start | bytes 61448 | tf_op jit(solution)/shard_map/ppermute | solution.py:197
  22.7 9.3 %collective-permute-start.2 = (bf16[16,640]{1,0:T(8,128)(2,1)S(1)}, bf16[16,640]{1,0:T(8,128)(2,1)S(1)}, u32[]{:S(2)}, u32[]{:S(2)}) collective-permute-start(bf16[16,640]{1,0:T(8,128)(2,1)S(1)} %get-tuple-element.32), channel_id=1, source_target_pairs={{0,1},{1,2},{2,3},{3,4},{4,5},{5,6},{6,7},{7,8},{8,9},{9,10},{10,1... | collective-permute-start | bytes 61448 | tf_op jit(solution)/shard_map/ppermute | solution.py:197
  27.3 7.1 %collective-permute-start = (f32[16,64]{1,0:T(8,128)S(1)}, f32[16,64]{1,0:T(8,128)S(1)}, u32[]{:S(2)}, u32[]{:S(2)}) collective-permute-start(f32[16,64]{1,0:T(8,128)S(1)} %get-tuple-element.26), channel_id=1, source_target_pairs={{16,32},{32,16},{17,33},{33,17},{18,34},{34,18},{19,35},{35,19},{2... | collective-permute-start | bytes 12296 | tf_op jit(solution)/shard_map/ppermute | solution.py:192

commit v3 on v2

--- a/solution.py
+++ b/solution.py
@@ -16,17 +16,19 @@
 LINE = 16
 PAIR = 2 * LINE
 LEADER = 11
-MEMBERS = [(1, LEADER), (0, LEADER)] + [(line, z) for z in [12, 10, 9, 8, 7, 6, 5, 4, 3, 2, 1, 0, 15, 14, 13] for line in range(2)]
+MEMBERS = [(1, LEADER)] + [(line, z) for line in (0, 1) for z in [12, 11, 10, 9, 8, 7, 6, 5, 4, 3, 2, 1, 0, 15, 14, 13] if (line, z) != (1, LEADER)]
 AXES = ("gx", "gy", "gz")
 EDGE = REACH * (LEAF + RANK)
 VMEM = pl.BlockSpec(memory_space=pltpu.VMEM)
 SMEM = pl.BlockSpec(memory_space=pltpu.SMEM)
 HBM = pl.BlockSpec(memory_space=pltpu.HBM)
-STAGED = 7
+STAGED = 5
 HELD = 2
 EARLY = 6
+FOLDED = 4
 NT = (((1,), (1,)), ((), ()))
 NN = (((1,), (0,)), ((), ()))
+TN = (((0,), (0,)), ((), ()))
 
 
 def dot(a, b, dims=NN):
@@ -40,51 +42,121 @@
     return both[: a.shape[0]] + both[a.shape[0] :]
 
 
+def dot_wide(a, b, dims=NN):
+    high = b.astype(jnp.bfloat16)
+    low = (b - high.astype(jnp.float32)).astype(jnp.bfloat16)
+    both = dot(a, jnp.concatenate([high, low], 1), dims)
+    return both[:, : b.shape[1]] + both[:, b.shape[1] :]
+
+
+def position():
+    spot = lax.axis_index("gz")
+    half = lax.axis_index("gy") & 1
+    return spot, half, half * LINE + spot
+
+
+def neighbours(h, spot, half, place):
+    count = PAIR >> h
+    q, low = place >> h, spot >> h
+    return [
+        (0, 0, jnp.maximum(q - 1, 0), q > 0),
+        (0, 1, jnp.minimum(q + 1, count - 1), q < count - 1),
+        (1, 0, count - 1, (half == 1) & (low == 0)),
+        (1, 1, 0, (half == 0) & (low == (LINE >> h) - 1)),
+    ]
+
+
+def fold(up_ref, coup_ref, folded_ref, maps):
+    spot, half, place = position()
+    maps[TOPL][...] = jnp.zeros_like(maps[TOPL])
+    down = [None]
+    for h in range(1, TOPL + 1):
+        step = up_ref[h - 1, (spot >> (h - 1)) & 1]
+        down.append(step.T.astype(jnp.float32) if h == 1 else dot_wide(step, down[-1], TN))
+    zero = jnp.zeros((RANK, RANK), jnp.float32)
+    for h in range(TOPL, -1, -1):
+        for to, side, q, used in neighbours(h, spot, half, place):
+            mat = coup_ref[h, side]
+            term = dot_wide(mat, down[h]) if h else mat.astype(jnp.float32)
+            term = term * used.astype(jnp.float32)
+            maps[h][q] += jnp.concatenate([zero, term] if to else [term, zero], 1)
+        if h:
+            mat = up_ref[h - 1].reshape(2 * RANK, RANK)
+            for q in range(PAIR >> h):
+                maps[h - 1][2 * q : 2 * q + 2] = dot_wide(mat, maps[h][q]).reshape(2, RANK, 2 * RANK)
+    for j, (line, z) in enumerate(MEMBERS):
+        values = maps[0][line * LINE + z]
+        high = values.astype(jnp.bfloat16)
+        at = slice(j * RANK, (j + 1) * RANK)
+        folded_ref[0, at, :] = high
+        folded_ref[1, at, :] = (values - high.astype(jnp.float32)).astype(jnp.bfloat16)
+
+
 def hold(staged, kept, done):
     return [pltpu.make_async_copy(staged[i], kept[i], done.at[i]) for i in range(HELD)]
 
 
+def levels_copies(up_hbm, coup_hbm, up_ref, coup_ref, done):
+    return [
+        pltpu.make_async_copy(up_hbm, up_ref, done.at[0]),
+        pltpu.make_async_copy(coup_hbm, coup_ref, done.at[1]),
+    ]
+
+
 def coeff_kernel(*refs):
     count = STAGED + HELD
-    staged, coeffs_ref, sends_ref, head_ref, tail_ref = refs[:count], *refs[count : count + 4]
-    kept, done, held = refs[count + 4 : -2], refs[-2], refs[-1]
+    staged, (up_hbm, coup_hbm), refs = refs[:count], refs[count : count + 2], refs[count + 2 :]
+    coeffs_ref, sends_ref, first_ref, second_ref, folded_ref = refs[:5]
+    kept, (done, held, mats), refs = refs[5 : count + 5], refs[count + 5 : count + 8], refs[count + 8 :]
+    up_ref, coup_ref, maps = refs[0], refs[1], refs[2:]
+    spot = lax.axis_index("gz")
+    early, folding = spot < EARLY, spot < FOLDED
     copies = [
         pltpu.make_async_copy(staged[i], kept[i], done.at[i]) for i in range(STAGED)
     ]
     for copy in copies:
         copy.start()
-    early = lax.axis_index("gz") < EARLY
 
     @pl.when(early)
     def _():
         for copy in hold(staged[STAGED:], kept[STAGED:], held):
             copy.start()
 
+    @pl.when(folding)
+    def _():
+        for copy in levels_copies(up_hbm, coup_hbm, up_ref, coup_ref, mats):
+            copy.start()
+
     rhs_ref, basis_ref, transfer_ref = kept[:3]
     copies[0].wait()
-    wide = REACH * LEAF
-    tail_ref[:, :wide] = rhs_ref[:, (LEAF_DEV - REACH) * LEAF :]
-    head_ref[:, :wide] = rhs_ref[:, :wide]
     copies[1].wait()
     parts = []
     for t in range(LEAF_DEV):
         block = rhs_ref[:, t * LEAF : (t + 1) * LEAF]
         parts.append(dot(block, basis_ref[t], NT).astype(jnp.bfloat16))
     copies[2].wait()
-    root = dot(parts[0], transfer_ref[0])
-    for t in range(1, LEAF_DEV):
-        root = root + dot(parts[t], transfer_ref[t])
+    coeffs = jnp.concatenate(parts, 1)
+    root = dot(coeffs, transfer_ref[...].reshape(LEAF_DEV * RANK, RANK))
     packed = jnp.concatenate([root[:8], root[8:]], 1)
     packed = jnp.concatenate([packed, packed], 0).astype(jnp.bfloat16)
     for j in range(PAIR // 2):
         sends_ref[16 * j : 16 * (j + 1), :] = packed
-    coeffs = jnp.concatenate(parts, 1)
     coeffs_ref[...] = coeffs
-    tail_ref[:, wide:] = coeffs[:, (LEAF_DEV - REACH) * RANK :]
-    head_ref[:, wide:] = coeffs[:, : REACH * RANK]
+    wide = REACH * LEAF
+    tail = jnp.concatenate([rhs_ref[:, (LEAF_DEV - REACH) * LEAF :], coeffs[:, (LEAF_DEV - REACH) * RANK :]], 1)
+    head = jnp.concatenate([rhs_ref[:, :wide], coeffs[:, : REACH * RANK]], 1)
+    odd = jnp.broadcast_to(spot & 1, tail.shape) == 1
+    first_ref[...] = jnp.where(odd, tail, head)
+    second_ref[...] = jnp.where(odd, head, tail)
     for copy in copies[3:]:
         copy.wait()
 
+    @pl.when(folding)
+    def _():
+        for copy in levels_copies(up_hbm, coup_hbm, up_ref, coup_ref, mats):
+            copy.wait()
+        fold(up_ref, coup_ref, folded_ref, maps)
+
     @pl.when(early)
     def _():
         for copy in hold(staged[STAGED:], kept[STAGED:], held):
@@ -92,7 +164,7 @@
 
 
 def near_kernel(
-    near_src, coup_src, rhs_ref, coeffs_ref, upper_ref, lower_ref, coupling_hbm, tiles_hbm,
+    near_src, coup_src, rhs_ref, coeffs_ref, first_ref, second_ref, coupling_hbm, tiles_hbm,
     coupling_in, tiles_in, near_ref, field_ref, coupling_ref, tiles_ref, blocks, leaf_coeffs, held,
 ):
     late = lax.axis_index("gz") >= EARLY
@@ -106,11 +178,12 @@
     anchor = own - REACH
     none = LEAF_DEV + 2 * REACH
     wide = REACH * LEAF
-    for i in range(REACH):
-        blocks[i] = lower_ref[:, i * LEAF : (i + 1) * LEAF]
-        blocks[REACH + LEAF_DEV + i] = upper_ref[:, i * LEAF : (i + 1) * LEAF]
-        leaf_coeffs[i] = lower_ref[:, wide + i * RANK : wide + (i + 1) * RANK]
-        leaf_coeffs[REACH + LEAF_DEV + i] = upper_ref[:, wide + i * RANK : wide + (i + 1) * RANK]
+    above = REACH + LEAF_DEV
+    odd = lax.axis_index("gz") & 1
+    for side_ref, start in ((first_ref, above * odd), (second_ref, above * (1 - odd))):
+        for i in range(REACH):
+            blocks[start + i] = side_ref[:, i * LEAF : (i + 1) * LEAF]
+            leaf_coeffs[start + i] = side_ref[:, wide + i * RANK : wide + (i + 1) * RANK]
     for t in range(LEAF_DEV):
         blocks[REACH + t] = rhs_ref[:, t * LEAF : (t + 1) * LEAF]
         leaf_coeffs[REACH + t] = coeffs_ref[:, t * RANK : (t + 1) * RANK]
@@ -134,11 +207,34 @@
     field_ref[...] = jnp.concatenate(fields, 1)
 
 
-def tree_kernel(got_ref, up_ref, coup_ref, own_ref, cross_ref, *levels):
-    spot = lax.axis_index("gz")
-    half = lax.axis_index("gy") & 1
-    place = half * LINE + spot
+def tree_kernel(got_ref, folded_ref, up_hbm, coup_hbm, own_ref, cross_ref, up_ref, coup_ref, mats, *levels):
+    spot, half, place = position()
     wide = got_ref[...].astype(jnp.float32).reshape(PAIR, 8, 2 * RANK)
+
+    @pl.when(spot < FOLDED)
+    def _():
+        parts = []
+        for j in range(0, PAIR, 2):
+            top = jnp.concatenate([wide[j, :, :RANK], wide[j + 1, :, :RANK]], 1)
+            low = jnp.concatenate([wide[j, :, RANK:], wide[j + 1, :, RANK:]], 1)
+            parts.append(jnp.concatenate([top, low], 0).astype(jnp.bfloat16))
+        given = jnp.concatenate(parts, 1)
+        both = dot(given, folded_ref[0]) + dot(given, folded_ref[1])
+        own_ref[...] = both[:, :RANK]
+        cross_ref[...] = both[:, RANK:]
+
+    @pl.when(spot >= FOLDED)
+    def _():
+        copies = levels_copies(up_hbm, coup_hbm, up_ref, coup_ref, mats)
+        for copy in copies:
+            copy.start()
+        for copy in copies:
+            copy.wait()
+        climb(wide, up_ref, coup_ref, own_ref, cross_ref, levels)
+
+
+def climb(wide, up_ref, coup_ref, own_ref, cross_ref, levels):
+    spot, half, place = position()
     for j, (line, z) in enumerate(MEMBERS):
         levels[0][0, line * LINE + z] = wide[j, :, :RANK]
         levels[0][1, line * LINE + z] = wide[j, :, RANK:]
@@ -149,19 +245,11 @@
         mat = up_ref[h - 1].reshape(2 * RANK, RANK)
         levels[h][...] = dot_split(pairs.reshape(NRHS * count, 2 * RANK), mat).reshape(2, count, 8, RANK)
 
-    def cluster(h, q, used):
-        return levels[h][:, q].reshape(NRHS, RANK) * used.astype(jnp.float32)
-
     fields = []
     for h in range(TOPL + 1):
-        count = PAIR >> h
-        q = place >> h
-        low = spot >> h
         sides = [
-            cluster(h, jnp.maximum(q - 1, 0), q > 0),
-            cluster(h, jnp.minimum(q + 1, count - 1), q < count - 1),
-            cluster(h, count - 1, (half == 1) & (low == 0)),
-            cluster(h, 0, (half == 0) & (low == (LINE >> h) - 1)),
+            levels[h][:, q].reshape(NRHS, RANK) * used.astype(jnp.float32)
+            for _, _, q, used in neighbours(h, spot, half, place)
         ]
         rows = jnp.concatenate([jnp.concatenate(sides[:2], 1), jnp.concatenate(sides[2:], 1)], 0)
         fields.append(dot_split(rows, coup_ref[h].reshape(2 * RANK, RANK)))
@@ -192,8 +280,10 @@
     return lax.ppermute(values, AXES, route)
 
 
-def shifted(values, count, distance):
-    route = [(i, i + distance) for i in range(count) if 0 <= i + distance < count]
+def traded(values, count, odd):
+    route = []
+    for low in range(odd, count - 1, 2):
+        route += [(low, low + 1), (low + 1, low)]
     return lax.ppermute(values, AXES, route)
 
 
@@ -227,34 +317,37 @@
     width = LEAF_DEV * LEAF
     ranks = LEAF_DEV * RANK
     inputs = (
-        rhs, leaf_basis, leaf_transfer, top_transfer, cluster_coupling,
-        near_sources, coupling_sources, leaf_coupling, near_tiles,
+        rhs, leaf_basis, leaf_transfer, near_sources, coupling_sources,
+        leaf_coupling, near_tiles, top_transfer, cluster_coupling,
     )
     inputs = [pltpu.with_memory_space_constraint(x, pltpu.HBM) for x in inputs]
-    coeffs, sends, head, tail, *kept = call(
+    coeffs, sends, first, second, folded, *kept = call(
         coeff_kernel,
         [
             ((NRHS, ranks), bf16),
             ((PAIR * 8, 2 * RANK), bf16),
             ((NRHS, EDGE), bf16),
             ((NRHS, EDGE), bf16),
+            ((2, PAIR * RANK, 2 * RANK), bf16),
         ]
-        + [(x.shape, x.dtype) for x in inputs],
-        scratch=[pltpu.SemaphoreType.DMA((STAGED,)), pltpu.SemaphoreType.DMA((HELD,))],
-        ins=[HBM] * (STAGED + HELD),
+        + [(x.shape, x.dtype) for x in inputs[:-2]],
+        scratch=[pltpu.SemaphoreType.DMA((n,)) for n in (STAGED, HELD, 2)]
+        + [pltpu.VMEM(x.shape, bf16) for x in inputs[-2:]]
+        + [pltpu.VMEM((PAIR >> h, RANK, 2 * RANK), f32) for h in range(TOPL + 1)],
+        ins=[HBM] * len(inputs),
         flops=2 * NRHS * ranks * (LEAF + RANK),
         moved=2**21,
         name="coeffs",
     )(*inputs)
-    rhs, leaf_basis, leaf_transfer, top_transfer, cluster_coupling = kept[:5]
-    near_sources, coupling_sources, coupling_kept, tiles_kept = kept[5:]
+    rhs, leaf_basis, leaf_transfer, near_sources, coupling_sources = kept[:STAGED]
+    coupling_kept, tiles_kept = kept[STAGED:]
     pairs = [
         [(2 * k + line) * LINE + z for line, z in MEMBERS]
         for k in range(lax.axis_size("gy") // 2)
     ]
     got = lax.all_to_all(sends, ("gy", "gz"), 0, 0, tiled=True, axis_index_groups=pairs)
-    upper = shifted(head, count, -1)
-    lower = shifted(tail, count, 1)
+    first = traded(first, count, 1)
+    second = traded(second, count, 0)
     near, field, _, _ = call(
         near_kernel,
         [((NRHS, width), f32), ((NRHS, ranks), f32)]
@@ -269,16 +362,18 @@
         flops=2 * NRHS * LEAF_DEV * (NEAR * LEAF * LEAF + ADM * RANK * RANK),
         moved=2**21,
         name="near",
-    )(near_sources, coupling_sources, rhs, coeffs, upper, lower, *inputs[-HELD:], coupling_kept, tiles_kept)
+    )(near_sources, coupling_sources, rhs, coeffs, first, second, *inputs[STAGED:-2], coupling_kept, tiles_kept)
     own, cross = call(
         tree_kernel,
         [((NRHS, RANK), f32)] * 2,
-        scratch=[pltpu.VMEM((2, PAIR >> h, 8, RANK), f32) for h in range(TOPL + 1)],
-        ins=[VMEM] * 3,
+        scratch=[pltpu.VMEM(x.shape, bf16) for x in inputs[-2:]]
+        + [pltpu.SemaphoreType.DMA((2,))]
+        + [pltpu.VMEM((2, PAIR >> h, 8, RANK), f32) for h in range(TOPL + 1)],
+        ins=[VMEM] * 2 + [HBM] * 2,
         flops=2**23,
         moved=2**18,
         name="tree",
-    )(got, top_transfer, cluster_coupling)
+    )(got, folded, *inputs[-2:])
     cross = crossed(cross, count)
     return call(
         out_kernel,

time: 35.8 us -> 35.3 us (0.986)
  starting transfers between devices: 26.1 us -> 24.3 us
  Pallas kernels: 6.24 us -> 7.76 us
    pallas_call x1, Pallas kernels: 2.53 us -> 5.22 us  [local(): call(coeff_kernel, [((NRHS, ranks), bf16), ((PAIR * 8, 2 * RANK), bf16),...]
    all_to_all x1, starting transfers between devices: 16.8 us -> 14.6 us  [local(): lax.all_to_all(sends, ('gy', 'gz'), 0, 0, tiled=True, axis_index_groups=p...]
    ppermute x1, waiting for transfers between devices: 1.25 us -> 2.94 us  [crossed(): return lax.ppermute(values, AXES, route)]
    ppermute x2, waiting for transfers between devices: 1.27 us -> 0.01 us  [traded(): return lax.ppermute(values, AXES, route)]
    pallas_call x1, Pallas kernels: 1.58 us -> 0.41 us  [local(): call(tree_kernel, [((NRHS, RANK), f32)] * 2, scratch=[pltpu.VMEM(x.shape,...]
    ppermute x2, starting transfers between devices: 5.84 us -> 6.74 us  [traded(): return lax.ppermute(values, AXES, route)]
    ppermute x1, starting transfers between devices: 3.42 us -> 2.96 us  [crossed(): return lax.ppermute(values, AXES, route)]
    all_to_all x1, waiting for transfers between devices: 0.43 us -> 0.01 us  [local(): lax.all_to_all(sends, ('gy', 'gz'), 0, 0, tiled=True, axis_index_groups=p...]
  transfers between devices with their start and end apart: 4 -> 4, of which waited for: 3 -> 1; matrix products, arithmetic and copies ran while one was open for 0% -> 0% of each run, Pallas kernels for 8% -> 4%
where the time goes in v3:
time: 35.3 us; the launch traced here: 35 us
  starting transfers between devices  24.3 us (69%)
  Pallas kernels  7.76 us (22%)
  waiting for transfers between devices  2.95 us (8%)
    all_to_all x1, starting transfers between devices, local(): lax.all_to_all(sends, ('gy', 'gz'), 0, 0, tiled=True, axis_index_groups=p...  14.6 us
    ppermute x2, starting transfers between devices, traded(): return lax.ppermute(values, AXES, route)  6.74 us
    pallas_call x1, Pallas kernels, local(): call(coeff_kernel, [((NRHS, ranks), bf16), ((PAIR * 8, 2 * RANK), bf16),...  5.22 us
    ppermute x1, starting transfers between devices, crossed(): return lax.ppermute(values, AXES, route)  2.96 us
    ppermute x1, waiting for transfers between devices, crossed(): return lax.ppermute(values, AXES, route)  2.94 us
    pallas_call x1, Pallas kernels, local(): call(near_kernel, [((NRHS, width), f32), ((NRHS, ranks), f32)] + [(x.shap...  1.15 us
    pallas_call x1, Pallas kernels, local(): call(out_kernel, [((NRHS, width), bf16)], ins=[VMEM] * 6, flops=2 * NRHS...  0.98 us
  transfers between devices with their start and end apart: 4, of which 1 were waited for; matrix products, arithmetic and copies ran while one was open for 0% of the time, Pallas kernels for 4%

profile of v3, /device:TPU:6, one launch (start us, length us, event | category | flops | bytes accessed | tf_op | source)
XLA Modules:
  0.0 35.0 jit_solution(13124956281972901035)
XLA Ops:
  0.0 5.2 %coeffs.1 = (bf16[16,256]{1,0:T(8,128)(2,1)S(1)}, bf16[256,128]{1,0:T(8,128)(2,1)}, bf16[16,640]{1,0:T(8,128)(2,1)S(1)}, bf16[16,640]{1,0:T(8,128)(2,1)S(1)}, bf...) custom-call(bf16[16,1024]{1,0:T(8,128)(2,1)} %refs_0_.1, ...), custom_call_target="tpu_custom_call" | custom-call | flops 2621440 | bytes 2097152 | tf_op jit(solution)/shard_map/coeffs/pallas_call | solution.py:324
  5.2 14.6 %all-to-all-start = ((bf16[32,8,128]{2,1,0:T(8,128)(2,1)}), bf16[32,8,128]{2,1,0:T(8,128)(2,1)S(1)}, u32[]{:S(2)}, u32[]{:S(2)}) async-start(bf16[32,8,128]{2,1,0:T(8,128)(2,1)} %bitcast), calls=%async_computation | async-start | bytes 131072 | tf_op jit(solution)/shard_map/all_to_all | solution.py:348
  19.8 3.3 %collective-permute-start.1 = (bf16[16,640]{1,0:T(8,128)(2,1)S(1)}, bf16[16,640]{1,0:T(8,128)(2,1)S(1)}, u32[]{:S(2)}, u32[]{:S(2)}) collective-permute-start(bf16[16,640]{1,0:T(8,128)(2,1)S(1)} %get-tuple-element.29), channel_id=1, source_target_pairs={{1,2},{2,1},{3,4},{4,3},{5,6},{6,5},{7,8},{8,7},{9,10},{10,9},{11,... | collective-permute-start | bytes 61448 | tf_op jit(solution)/shard_map/ppermute | solution.py:287
  23.1 3.4 %collective-permute-start.2 = (bf16[16,640]{1,0:T(8,128)(2,1)S(1)}, bf16[16,640]{1,0:T(8,128)(2,1)S(1)}, u32[]{:S(2)}, u32[]{:S(2)}) collective-permute-start(bf16[16,640]{1,0:T(8,128)(2,1)S(1)} %get-tuple-element.30), channel_id=1, source_target_pairs={{0,1},{1,0},{2,3},{3,2},{4,5},{5,4},{6,7},{7,6},{8,9},{9,8},{10,11... | collective-permute-start | bytes 61448 | tf_op jit(solution)/shard_map/ppermute | solution.py:287
  26.6 0.0 all-to-all-done
  26.6 0.4 %tree.1 = (f32[16,64]{1,0:T(8,128)S(1)}, f32[16,64]{1,0:T(8,128)S(1)}) custom-call(bf16[256,128]{1,0:T(8,128)(2,1)S(1)} %bitcast.2, bf16[2,2048,128]{2,1,0:T(8,128)(2,1)S(1)} %get-tuple-element.22.folded_ref, bf16[4,2,64,64]{3,2,1,0:T(8,128)(2,1)} %up_hbm.1, bf16[5,2,64,64]{3,2,1,0:T(8,128)(2,1)} %coup_hbm.1), custom_call_target="tpu_custom_call" | custom-call | flops 8388608 | bytes 262144 | tf_op jit(solution)/shard_map/tree/pallas_call | solution.py:366
  27.0 3.0 %collective-permute-start = (f32[16,64]{1,0:T(8,128)S(1)}, f32[16,64]{1,0:T(8,128)S(1)}, u32[]{:S(2)}, u32[]{:S(2)}) collective-permute-start(f32[16,64]{1,0:T(8,128)S(1)} %get-tuple-element.24), channel_id=1, source_target_pairs={{16,32},{32,16},{17,33},{33,17},{18,34},{34,18},{19,35},{35,19},{2... | collective-permute-start | bytes 12296 | tf_op jit(solution)/shard_map/ppermute | solution.py:280
  29.9 0.0 collective-permute-done.1.first_ref
  30.0 0.0 collective-permute-done.2.second_ref
  30.0 1.1 %near.1 = (f32[16,1024]{1,0:T(8,128)S(1)}, f32[16,256]{1,0:T(8,128)S(1)}, bf16[4,6,64,64]{3,2,1,0:T(8,128)(2,1)S(1)}, bf16[4,3,256,256]{3,2,1,0:T(8,128)(2,1)S(1)}) custom-call(s32[4,3]{1,0:T(4,128)S(1)} %get-tuple-element.25.near_src, s32[4,6]{1,0:T(4,128)S(1)} %get-tuple-element.26.coup_src, ...), custom_call_target="tpu_custom_call", output_to_operand_aliasing={{2}: (8, {}), {3}: (9, {})} | custom-call | flops 28311552 | bytes 2097152 | tf_op jit(solution)/shard_map/near/pallas_call | solution.py:351
  31.1 2.9 %collective-permute-done.cross_ref = f32[16,64]{1,0:T(8,128)S(1)} collective-permute-done((f32[16,64]{1,0:T(8,128)S(1)}, f32[16,64]{1,0:T(8,128)S(1)}, u32[]{:S(2)}, u32[]{:S(2)}) %collective-permute-start) | collective-permute-done | bytes 4128 | tf_op jit(solution)/shard_map/ppermute | solution.py:280
  34.1 1.0 %out.1 = bf16[16,1024]{1,0:T(8,128)(2,1)} custom-call(f32[16,64]{1,0:T(8,128)S(1)} %get-tuple-element.23.own_ref, f32[16,64]{1,0:T(8,128)S(1)} %collective-permute-done.cross_ref, f32[16,256]{1,0:T(8,128)S(1)} %get-tuple-element.33.field_ref, f32[16,1024]{1,0:T(8,128)S(1)} %get-tuple-element.34.near_ref, ...), custom_call_target="tpu_custom_call" | custom-call | flops 2621440 | bytes 262144 | tf_op jit(solution)/shard_map/out/pallas_call | solution.py:378
Async XLA Ops:
  5.2 21.3 %all-to-all-start = ((bf16[32,8,128]{2,1,0:T(8,128)(2,1)}), bf16[32,8,128]{2,1,0:T(8,128)(2,1)S(1)}, u32[]{:S(2)}, u32[]{:S(2)}) async-start(bf16[32,8,128]{2,1,0:T(8,128)(2,1)} %bitcast), calls=%async_computation | async-start | bytes 131072 | tf_op jit(solution)/shard_map/all_to_all | solution.py:348
  19.8 10.1 %collective-permute-start.1 = (bf16[16,640]{1,0:T(8,128)(2,1)S(1)}, bf16[16,640]{1,0:T(8,128)(2,1)S(1)}, u32[]{:S(2)}, u32[]{:S(2)}) collective-permute-start(bf16[16,640]{1,0:T(8,128)(2,1)S(1)} %get-tuple-element.29), channel_id=1, source_target_pairs={{1,2},{2,1},{3,4},{4,3},{5,6},{6,5},{7,8},{8,7},{9,10},{10,9},{11,... | collective-permute-start | bytes 61448 | tf_op jit(solution)/shard_map/ppermute | solution.py:287
  23.1 6.8 %collective-permute-start.2 = (bf16[16,640]{1,0:T(8,128)(2,1)S(1)}, bf16[16,640]{1,0:T(8,128)(2,1)S(1)}, u32[]{:S(2)}, u32[]{:S(2)}) collective-permute-start(bf16[16,640]{1,0:T(8,128)(2,1)S(1)} %get-tuple-element.30), channel_id=1, source_target_pairs={{0,1},{1,0},{2,3},{3,2},{4,5},{5,4},{6,7},{7,6},{8,9},{9,8},{10,11... | collective-permute-start | bytes 61448 | tf_op jit(solution)/shard_map/ppermute | solution.py:287
  27.0 7.1 %collective-permute-start = (f32[16,64]{1,0:T(8,128)S(1)}, f32[16,64]{1,0:T(8,128)S(1)}, u32[]{:S(2)}, u32[]{:S(2)}) collective-permute-start(f32[16,64]{1,0:T(8,128)S(1)} %get-tuple-element.24), channel_id=1, source_target_pairs={{16,32},{32,16},{17,33},{33,17},{18,34},{34,18},{19,35},{35,19},{2... | collective-permute-start | bytes 12296 | tf_op jit(solution)/shard_map/ppermute | solution.py:280

commit v4 on v3

--- a/solution.py
+++ b/solution.py
@@ -106,9 +106,9 @@
 def coeff_kernel(*refs):
     count = STAGED + HELD
     staged, (up_hbm, coup_hbm), refs = refs[:count], refs[count : count + 2], refs[count + 2 :]
-    coeffs_ref, sends_ref, first_ref, second_ref, folded_ref = refs[:5]
+    coeffs_ref, sends_hbm, first_ref, second_ref, folded_ref = refs[:5]
     kept, (done, held, mats), refs = refs[5 : count + 5], refs[count + 5 : count + 8], refs[count + 8 :]
-    up_ref, coup_ref, maps = refs[0], refs[1], refs[2:]
+    up_ref, coup_ref, sends_ref, sent, maps = *refs[:4], refs[4:]
     spot = lax.axis_index("gz")
     early, folding = spot < EARLY, spot < FOLDED
     copies = [
@@ -141,6 +141,8 @@
     packed = jnp.concatenate([packed, packed], 0).astype(jnp.bfloat16)
     for j in range(PAIR // 2):
         sends_ref[16 * j : 16 * (j + 1), :] = packed
+    sending = pltpu.make_async_copy(sends_ref, sends_hbm, sent.at[0])
+    sending.start()
     coeffs_ref[...] = coeffs
     wide = REACH * LEAF
     tail = jnp.concatenate([rhs_ref[:, (LEAF_DEV - REACH) * LEAF :], coeffs[:, (LEAF_DEV - REACH) * RANK :]], 1)
@@ -150,6 +152,7 @@
     second_ref[...] = jnp.where(odd, head, tail)
     for copy in copies[3:]:
         copy.wait()
+    sending.wait()
 
     @pl.when(folding)
     def _():
@@ -287,12 +290,12 @@
     return lax.ppermute(values, AXES, route)
 
 
-def call(kernel, outs, scratch=(), ins=(), flops=0, moved=0, name=None, aliases=None):
+def call(kernel, outs, scratch=(), ins=(), flops=0, moved=0, name=None, aliases=None, hbm=()):
     return pl.pallas_call(
         kernel,
         out_shape=[jax.ShapeDtypeStruct(shape, dtype) for shape, dtype in outs],
         in_specs=list(ins),
-        out_specs=[VMEM] * len(outs),
+        out_specs=[HBM if i in hbm else VMEM for i in range(len(outs))],
         scratch_shapes=list(scratch),
         cost_estimate=pl.CostEstimate(flops=flops, bytes_accessed=moved, transcendentals=0),
         compiler_params=pltpu.CompilerParams(vmem_limit_bytes=24 * 2**20),
@@ -333,8 +336,10 @@
         + [(x.shape, x.dtype) for x in inputs[:-2]],
         scratch=[pltpu.SemaphoreType.DMA((n,)) for n in (STAGED, HELD, 2)]
         + [pltpu.VMEM(x.shape, bf16) for x in inputs[-2:]]
+        + [pltpu.VMEM((PAIR * 8, 2 * RANK), bf16), pltpu.SemaphoreType.DMA((1,))]
         + [pltpu.VMEM((PAIR >> h, RANK, 2 * RANK), f32) for h in range(TOPL + 1)],
         ins=[HBM] * len(inputs),
+        hbm=[1],
         flops=2 * NRHS * ranks * (LEAF + RANK),
         moved=2**21,
         name="coeffs",

time: 35.3 us -> 35 us (level)
  no operation moved by 1% of the time
where the time goes in v4:
time: 35 us; the launch traced here: 34.7 us
  starting transfers between devices  24.3 us (69%)
  Pallas kernels  7.41 us (21%)
  waiting for transfers between devices  2.95 us (8%)
    all_to_all x1, starting transfers between devices, local(): lax.all_to_all(sends, ('gy', 'gz'), 0, 0, tiled=True, axis_index_groups=p...  14.6 us
    ppermute x2, starting transfers between devices, traded(): return lax.ppermute(values, AXES, route)  6.74 us
    pallas_call x1, Pallas kernels, local(): call(coeff_kernel, [((NRHS, ranks), bf16), ((PAIR * 8, 2 * RANK), bf16),...  4.88 us
    ppermute x1, starting transfers between devices, crossed(): return lax.ppermute(values, AXES, route)  2.96 us
    ppermute x1, waiting for transfers between devices, crossed(): return lax.ppermute(values, AXES, route)  2.94 us
    pallas_call x1, Pallas kernels, local(): call(near_kernel, [((NRHS, width), f32), ((NRHS, ranks), f32)] + [(x.shap...  1.15 us
    pallas_call x1, Pallas kernels, local(): call(out_kernel, [((NRHS, width), bf16)], ins=[VMEM] * 6, flops=2 * NRHS...  0.98 us
  transfers between devices with their start and end apart: 4, of which 1 were waited for; matrix products, arithmetic and copies ran while one was open for 0% of the time, Pallas kernels for 4%

profile of v4, /device:TPU:6, one launch (start us, length us, event | category | flops | bytes accessed | tf_op | source)
XLA Modules:
  0.0 34.7 jit_solution(15038401918748606299)
XLA Ops:
  0.0 4.9 %coeffs.1 = (bf16[16,256]{1,0:T(8,128)(2,1)S(1)}, bf16[256,128]{1,0:T(8,128)(2,1)}, bf16[16,640]{1,0:T(8,128)(2,1)S(1)}, bf16[16,640]{1,0:T(8,128)(2,1)S(1)}, bf...) custom-call(bf16[16,1024]{1,0:T(8,128)(2,1)} %refs_0_.1, ...), custom_call_target="tpu_custom_call" | custom-call | flops 2621440 | bytes 2097152 | tf_op jit(solution)/shard_map/coeffs/pallas_call | solution.py:327
  4.9 14.6 %all-to-all-start = ((bf16[32,8,128]{2,1,0:T(8,128)(2,1)}), bf16[32,8,128]{2,1,0:T(8,128)(2,1)S(1)}, u32[]{:S(2)}, u32[]{:S(2)}) async-start(bf16[32,8,128]{2,1,0:T(8,128)(2,1)} %bitcast), calls=%async_computation | async-start | bytes 131072 | tf_op jit(solution)/shard_map/all_to_all | solution.py:353
  19.4 3.3 %collective-permute-start.1 = (bf16[16,640]{1,0:T(8,128)(2,1)S(1)}, bf16[16,640]{1,0:T(8,128)(2,1)S(1)}, u32[]{:S(2)}, u32[]{:S(2)}) collective-permute-start(bf16[16,640]{1,0:T(8,128)(2,1)S(1)} %get-tuple-element.29), channel_id=1, source_target_pairs={{1,2},{2,1},{3,4},{4,3},{5,6},{6,5},{7,8},{8,7},{9,10},{10,9},{11,... | collective-permute-start | bytes 61448 | tf_op jit(solution)/shard_map/ppermute | solution.py:290
  22.8 3.4 %collective-permute-start.2 = (bf16[16,640]{1,0:T(8,128)(2,1)S(1)}, bf16[16,640]{1,0:T(8,128)(2,1)S(1)}, u32[]{:S(2)}, u32[]{:S(2)}) collective-permute-start(bf16[16,640]{1,0:T(8,128)(2,1)S(1)} %get-tuple-element.30), channel_id=1, source_target_pairs={{0,1},{1,0},{2,3},{3,2},{4,5},{5,4},{6,7},{7,6},{8,9},{9,8},{10,11... | collective-permute-start | bytes 61448 | tf_op jit(solution)/shard_map/ppermute | solution.py:290
  26.2 0.0 all-to-all-done
  26.2 0.4 %tree.1 = (f32[16,64]{1,0:T(8,128)S(1)}, f32[16,64]{1,0:T(8,128)S(1)}) custom-call(bf16[256,128]{1,0:T(8,128)(2,1)S(1)} %bitcast.2, bf16[2,2048,128]{2,1,0:T(8,128)(2,1)S(1)} %get-tuple-element.22.folded_ref, bf16[4,2,64,64]{3,2,1,0:T(8,128)(2,1)} %up_hbm.1, bf16[5,2,64,64]{3,2,1,0:T(8,128)(2,1)} %coup_hbm.1), custom_call_target="tpu_custom_call" | custom-call | flops 8388608 | bytes 262144 | tf_op jit(solution)/shard_map/tree/pallas_call | solution.py:371
  26.6 3.0 %collective-permute-start = (f32[16,64]{1,0:T(8,128)S(1)}, f32[16,64]{1,0:T(8,128)S(1)}, u32[]{:S(2)}, u32[]{:S(2)}) collective-permute-start(f32[16,64]{1,0:T(8,128)S(1)} %get-tuple-element.24), channel_id=1, source_target_pairs={{16,32},{32,16},{17,33},{33,17},{18,34},{34,18},{19,35},{35,19},{2... | collective-permute-start | bytes 12296 | tf_op jit(solution)/shard_map/ppermute | solution.py:283
  29.6 0.0 collective-permute-done.1.first_ref
  29.6 0.0 collective-permute-done.2.second_ref
  29.6 1.1 %near.1 = (f32[16,1024]{1,0:T(8,128)S(1)}, f32[16,256]{1,0:T(8,128)S(1)}, bf16[4,6,64,64]{3,2,1,0:T(8,128)(2,1)S(1)}, bf16[4,3,256,256]{3,2,1,0:T(8,128)(2,1)S(1)}) custom-call(s32[4,3]{1,0:T(4,128)S(1)} %get-tuple-element.25.near_src, s32[4,6]{1,0:T(4,128)S(1)} %get-tuple-element.26.coup_src, ...), custom_call_target="tpu_custom_call", output_to_operand_aliasing={{2}: (8, {}), {3}: (9, {})} | custom-call | flops 28311552 | bytes 2097152 | tf_op jit(solution)/shard_map/near/pallas_call | solution.py:356
  30.8 2.9 %collective-permute-done.cross_ref = f32[16,64]{1,0:T(8,128)S(1)} collective-permute-done((f32[16,64]{1,0:T(8,128)S(1)}, f32[16,64]{1,0:T(8,128)S(1)}, u32[]{:S(2)}, u32[]{:S(2)}) %collective-permute-start) | collective-permute-done | bytes 4128 | tf_op jit(solution)/shard_map/ppermute | solution.py:283
  33.7 1.0 %out.1 = bf16[16,1024]{1,0:T(8,128)(2,1)} custom-call(f32[16,64]{1,0:T(8,128)S(1)} %get-tuple-element.23.own_ref, f32[16,64]{1,0:T(8,128)S(1)} %collective-permute-done.cross_ref, f32[16,256]{1,0:T(8,128)S(1)} %get-tuple-element.33.field_ref, f32[16,1024]{1,0:T(8,128)S(1)} %get-tuple-element.34.near_ref, ...), custom_call_target="tpu_custom_call" | custom-call | flops 2621440 | bytes 262144 | tf_op jit(solution)/shard_map/out/pallas_call | solution.py:383
Async XLA Ops:
  4.9 21.3 %all-to-all-start = ((bf16[32,8,128]{2,1,0:T(8,128)(2,1)}), bf16[32,8,128]{2,1,0:T(8,128)(2,1)S(1)}, u32[]{:S(2)}, u32[]{:S(2)}) async-start(bf16[32,8,128]{2,1,0:T(8,128)(2,1)} %bitcast), calls=%async_computation | async-start | bytes 131072 | tf_op jit(solution)/shard_map/all_to_all | solution.py:353
  19.4 10.1 %collective-permute-start.1 = (bf16[16,640]{1,0:T(8,128)(2,1)S(1)}, bf16[16,640]{1,0:T(8,128)(2,1)S(1)}, u32[]{:S(2)}, u32[]{:S(2)}) collective-permute-start(bf16[16,640]{1,0:T(8,128)(2,1)S(1)} %get-tuple-element.29), channel_id=1, source_target_pairs={{1,2},{2,1},{3,4},{4,3},{5,6},{6,5},{7,8},{8,7},{9,10},{10,9},{11,... | collective-permute-start | bytes 61448 | tf_op jit(solution)/shard_map/ppermute | solution.py:290
  22.8 6.8 %collective-permute-start.2 = (bf16[16,640]{1,0:T(8,128)(2,1)S(1)}, bf16[16,640]{1,0:T(8,128)(2,1)S(1)}, u32[]{:S(2)}, u32[]{:S(2)}) collective-permute-start(bf16[16,640]{1,0:T(8,128)(2,1)S(1)} %get-tuple-element.30), channel_id=1, source_target_pairs={{0,1},{1,0},{2,3},{3,2},{4,5},{5,4},{6,7},{7,6},{8,9},{9,8},{10,11... | collective-permute-start | bytes 61448 | tf_op jit(solution)/shard_map/ppermute | solution.py:290
  26.6 7.1 %collective-permute-start = (f32[16,64]{1,0:T(8,128)S(1)}, f32[16,64]{1,0:T(8,128)S(1)}, u32[]{:S(2)}, u32[]{:S(2)}) collective-permute-start(f32[16,64]{1,0:T(8,128)S(1)} %get-tuple-element.24), channel_id=1, source_target_pairs={{16,32},{32,16},{17,33},{33,17},{18,34},{34,18},{19,35},{35,19},{2... | collective-permute-start | bytes 12296 | tf_op jit(solution)/shard_map/ppermute | solution.py:283

commit v5 on v4

--- a/solution.py
+++ b/solution.py
@@ -114,8 +114,8 @@
     copies = [
         pltpu.make_async_copy(staged[i], kept[i], done.at[i]) for i in range(STAGED)
     ]
-    for copy in copies:
-        copy.start()
+    for i in (1, 0, 2):
+        copies[i].start()
 
     @pl.when(early)
     def _():
@@ -128,12 +128,14 @@
             copy.start()
 
     rhs_ref, basis_ref, transfer_ref = kept[:3]
+    copies[1].wait()
     copies[0].wait()
-    copies[1].wait()
     parts = []
     for t in range(LEAF_DEV):
         block = rhs_ref[:, t * LEAF : (t + 1) * LEAF]
         parts.append(dot(block, basis_ref[t], NT).astype(jnp.bfloat16))
+    for copy in copies[3:]:
+        copy.start()
     copies[2].wait()
     coeffs = jnp.concatenate(parts, 1)
     root = dot(coeffs, transfer_ref[...].reshape(LEAF_DEV * RANK, RANK))

time: 35 us -> 35 us (level)
  no operation moved by 1% of the time
where the time goes in v5:
time: 35 us; the launch traced here: 34.7 us
  starting transfers between devices  24.3 us (69%)
  Pallas kernels  7.38 us (21%)
  waiting for transfers between devices  2.94 us (8%)
    all_to_all x1, starting transfers between devices, local(): lax.all_to_all(sends, ('gy', 'gz'), 0, 0, tiled=True, axis_index_groups=p...  14.6 us
    ppermute x2, starting transfers between devices, traded(): return lax.ppermute(values, AXES, route)  6.74 us
    pallas_call x1, Pallas kernels, local(): call(coeff_kernel, [((NRHS, ranks), bf16), ((PAIR * 8, 2 * RANK), bf16),...  4.85 us
    ppermute x1, starting transfers between devices, crossed(): return lax.ppermute(values, AXES, route)  2.96 us
    ppermute x1, waiting for transfers between devices, crossed(): return lax.ppermute(values, AXES, route)  2.93 us
    pallas_call x1, Pallas kernels, local(): call(near_kernel, [((NRHS, width), f32), ((NRHS, ranks), f32)] + [(x.shap...  1.15 us
    pallas_call x1, Pallas kernels, local(): call(out_kernel, [((NRHS, width), bf16)], ins=[VMEM] * 6, flops=2 * NRHS...  0.98 us
  transfers between devices with their start and end apart: 4, of which 1 were waited for; matrix products, arithmetic and copies ran while one was open for 0% of the time, Pallas kernels for 4%

profile of v5, /device:TPU:6, one launch (start us, length us, event | category | flops | bytes accessed | tf_op | source)
XLA Modules:
  0.0 34.7 jit_solution(4481420122213482615)
XLA Ops:
  0.0 4.9 %coeffs.1 = (bf16[16,256]{1,0:T(8,128)(2,1)S(1)}, bf16[256,128]{1,0:T(8,128)(2,1)}, bf16[16,640]{1,0:T(8,128)(2,1)S(1)}, bf16[16,640]{1,0:T(8,128)(2,1)S(1)}, bf...) custom-call(bf16[16,1024]{1,0:T(8,128)(2,1)} %refs_0_.1, ...), custom_call_target="tpu_custom_call" | custom-call | flops 2621440 | bytes 2097152 | tf_op jit(solution)/shard_map/coeffs/pallas_call | solution.py:329
  4.9 14.6 %all-to-all-start = ((bf16[32,8,128]{2,1,0:T(8,128)(2,1)}), bf16[32,8,128]{2,1,0:T(8,128)(2,1)S(1)}, u32[]{:S(2)}, u32[]{:S(2)}) async-start(bf16[32,8,128]{2,1,0:T(8,128)(2,1)} %bitcast), calls=%async_computation | async-start | bytes 131072 | tf_op jit(solution)/shard_map/all_to_all | solution.py:355
  19.4 3.3 %collective-permute-start.1 = (bf16[16,640]{1,0:T(8,128)(2,1)S(1)}, bf16[16,640]{1,0:T(8,128)(2,1)S(1)}, u32[]{:S(2)}, u32[]{:S(2)}) collective-permute-start(bf16[16,640]{1,0:T(8,128)(2,1)S(1)} %get-tuple-element.29), channel_id=1, source_target_pairs={{1,2},{2,1},{3,4},{4,3},{5,6},{6,5},{7,8},{8,7},{9,10},{10,9},{11,... | collective-permute-start | bytes 61448 | tf_op jit(solution)/shard_map/ppermute | solution.py:292
  22.8 3.4 %collective-permute-start.2 = (bf16[16,640]{1,0:T(8,128)(2,1)S(1)}, bf16[16,640]{1,0:T(8,128)(2,1)S(1)}, u32[]{:S(2)}, u32[]{:S(2)}) collective-permute-start(bf16[16,640]{1,0:T(8,128)(2,1)S(1)} %get-tuple-element.30), channel_id=1, source_target_pairs={{0,1},{1,0},{2,3},{3,2},{4,5},{5,4},{6,7},{7,6},{8,9},{9,8},{10,11... | collective-permute-start | bytes 61448 | tf_op jit(solution)/shard_map/ppermute | solution.py:292
  26.2 0.0 all-to-all-done
  26.2 0.4 %tree.1 = (f32[16,64]{1,0:T(8,128)S(1)}, f32[16,64]{1,0:T(8,128)S(1)}) custom-call(bf16[256,128]{1,0:T(8,128)(2,1)S(1)} %bitcast.2, bf16[2,2048,128]{2,1,0:T(8,128)(2,1)S(1)} %get-tuple-element.22.folded_ref, bf16[4,2,64,64]{3,2,1,0:T(8,128)(2,1)} %up_hbm.1, bf16[5,2,64,64]{3,2,1,0:T(8,128)(2,1)} %coup_hbm.1), custom_call_target="tpu_custom_call" | custom-call | flops 8388608 | bytes 262144 | tf_op jit(solution)/shard_map/tree/pallas_call | solution.py:373
  26.6 3.0 %collective-permute-start = (f32[16,64]{1,0:T(8,128)S(1)}, f32[16,64]{1,0:T(8,128)S(1)}, u32[]{:S(2)}, u32[]{:S(2)}) collective-permute-start(f32[16,64]{1,0:T(8,128)S(1)} %get-tuple-element.24), channel_id=1, source_target_pairs={{16,32},{32,16},{17,33},{33,17},{18,34},{34,18},{19,35},{35,19},{2... | collective-permute-start | bytes 12296 | tf_op jit(solution)/shard_map/ppermute | solution.py:285
  29.6 0.0 collective-permute-done.1.first_ref
  29.6 0.0 collective-permute-done.2.second_ref
  29.6 1.1 %near.1 = (f32[16,1024]{1,0:T(8,128)S(1)}, f32[16,256]{1,0:T(8,128)S(1)}, bf16[4,6,64,64]{3,2,1,0:T(8,128)(2,1)S(1)}, bf16[4,3,256,256]{3,2,1,0:T(8,128)(2,1)S(1)}) custom-call(s32[4,3]{1,0:T(4,128)S(1)} %get-tuple-element.25.near_src, s32[4,6]{1,0:T(4,128)S(1)} %get-tuple-element.26.coup_src, ...), custom_call_target="tpu_custom_call", output_to_operand_aliasing={{2}: (8, {}), {3}: (9, {})} | custom-call | flops 28311552 | bytes 2097152 | tf_op jit(solution)/shard_map/near/pallas_call | solution.py:358
  30.8 2.9 %collective-permute-done.cross_ref = f32[16,64]{1,0:T(8,128)S(1)} collective-permute-done((f32[16,64]{1,0:T(8,128)S(1)}, f32[16,64]{1,0:T(8,128)S(1)}, u32[]{:S(2)}, u32[]{:S(2)}) %collective-permute-start) | collective-permute-done | bytes 4128 | tf_op jit(solution)/shard_map/ppermute | solution.py:285
  33.7 1.0 %out.1 = bf16[16,1024]{1,0:T(8,128)(2,1)} custom-call(f32[16,64]{1,0:T(8,128)S(1)} %get-tuple-element.23.own_ref, f32[16,64]{1,0:T(8,128)S(1)} %collective-permute-done.cross_ref, f32[16,256]{1,0:T(8,128)S(1)} %get-tuple-element.33.field_ref, f32[16,1024]{1,0:T(8,128)S(1)} %get-tuple-element.34.near_ref, ...), custom_call_target="tpu_custom_call" | custom-call | flops 2621440 | bytes 262144 | tf_op jit(solution)/shard_map/out/pallas_call | solution.py:385
Async XLA Ops:
  4.9 21.3 %all-to-all-start = ((bf16[32,8,128]{2,1,0:T(8,128)(2,1)}), bf16[32,8,128]{2,1,0:T(8,128)(2,1)S(1)}, u32[]{:S(2)}, u32[]{:S(2)}) async-start(bf16[32,8,128]{2,1,0:T(8,128)(2,1)} %bitcast), calls=%async_computation | async-start | bytes 131072 | tf_op jit(solution)/shard_map/all_to_all | solution.py:355
  19.4 10.2 %collective-permute-start.1 = (bf16[16,640]{1,0:T(8,128)(2,1)S(1)}, bf16[16,640]{1,0:T(8,128)(2,1)S(1)}, u32[]{:S(2)}, u32[]{:S(2)}) collective-permute-start(bf16[16,640]{1,0:T(8,128)(2,1)S(1)} %get-tuple-element.29), channel_id=1, source_target_pairs={{1,2},{2,1},{3,4},{4,3},{5,6},{6,5},{7,8},{8,7},{9,10},{10,9},{11,... | collective-permute-start | bytes 61448 | tf_op jit(solution)/shard_map/ppermute | solution.py:292
  22.8 6.8 %collective-permute-start.2 = (bf16[16,640]{1,0:T(8,128)(2,1)S(1)}, bf16[16,640]{1,0:T(8,128)(2,1)S(1)}, u32[]{:S(2)}, u32[]{:S(2)}) collective-permute-start(bf16[16,640]{1,0:T(8,128)(2,1)S(1)} %get-tuple-element.30), channel_id=1, source_target_pairs={{0,1},{1,0},{2,3},{3,2},{4,5},{5,4},{6,7},{7,6},{8,9},{9,8},{10,11... | collective-permute-start | bytes 61448 | tf_op jit(solution)/shard_map/ppermute | solution.py:292
  26.6 7.1 %collective-permute-start = (f32[16,64]{1,0:T(8,128)S(1)}, f32[16,64]{1,0:T(8,128)S(1)}, u32[]{:S(2)}, u32[]{:S(2)}) collective-permute-start(f32[16,64]{1,0:T(8,128)S(1)} %get-tuple-element.24), channel_id=1, source_target_pairs={{16,32},{32,16},{17,33},{33,17},{18,34},{34,18},{19,35},{35,19},{2... | collective-permute-start | bytes 12296 | tf_op jit(solution)/shard_map/ppermute | solution.py:285

commit v6 on v4

--- a/solution.py
+++ b/solution.py
@@ -224,7 +224,7 @@
         given = jnp.concatenate(parts, 1)
         both = dot(given, folded_ref[0]) + dot(given, folded_ref[1])
         own_ref[...] = both[:, :RANK]
-        cross_ref[...] = both[:, RANK:]
+        cross_ref[...] = jnp.concatenate([both[:8, RANK:], both[8:, RANK:]], 1)
 
     @pl.when(spot >= FOLDED)
     def _():
@@ -261,11 +261,12 @@
         parity = (spot >> (h - 1)) & 1
         incoming = fields[h - 1] + dot_split(incoming, up_ref[h - 1, parity], NT)
     own_ref[...] = incoming[:NRHS]
-    cross_ref[...] = incoming[NRHS:]
+    cross_ref[...] = jnp.concatenate([incoming[NRHS : NRHS + 8], incoming[NRHS + 8 :]], 1)
 
 
 def out_kernel(own_ref, cross_ref, field_ref, near_ref, transfer_ref, basis_ref, out_ref):
-    incoming = own_ref[...] + cross_ref[...]
+    cross = cross_ref[...]
+    incoming = own_ref[...] + jnp.concatenate([cross[:, :RANK], cross[:, RANK:]], 0)
     spread = dot_split(incoming, transfer_ref[...].reshape(LEAF_DEV * RANK, RANK), NT)
     potential = (field_ref[...] + spread).astype(jnp.bfloat16)
     for t in range(LEAF_DEV):
@@ -370,7 +371,7 @@
     )(near_sources, coupling_sources, rhs, coeffs, first, second, *inputs[STAGED:-2], coupling_kept, tiles_kept)
     own, cross = call(
         tree_kernel,
-        [((NRHS, RANK), f32)] * 2,
+        [((NRHS, RANK), f32), ((8, 2 * RANK), f32)],
         scratch=[pltpu.VMEM(x.shape, bf16) for x in inputs[-2:]]
         + [pltpu.SemaphoreType.DMA((2,))]
         + [pltpu.VMEM((2, PAIR >> h, 8, RANK), f32) for h in range(TOPL + 1)],

time: 35 us -> 35 us (level)
  no operation moved by 1% of the time
where the time goes in v6:
time: 35 us; the launch traced here: 34.7 us
  starting transfers between devices  24.3 us (69%)
  Pallas kernels  7.44 us (21%)
  waiting for transfers between devices  2.9 us (8%)
    all_to_all x1, starting transfers between devices, local(): lax.all_to_all(sends, ('gy', 'gz'), 0, 0, tiled=True, axis_index_groups=p...  14.6 us
    ppermute x2, starting transfers between devices, traded(): return lax.ppermute(values, AXES, route)  6.74 us
    pallas_call x1, Pallas kernels, local(): call(coeff_kernel, [((NRHS, ranks), bf16), ((PAIR * 8, 2 * RANK), bf16),...  4.88 us
    ppermute x1, starting transfers between devices, crossed(): return lax.ppermute(values, AXES, route)  2.96 us
    ppermute x1, waiting for transfers between devices, crossed(): return lax.ppermute(values, AXES, route)  2.89 us
    pallas_call x1, Pallas kernels, local(): call(near_kernel, [((NRHS, width), f32), ((NRHS, ranks), f32)] + [(x.shap...  1.15 us
    pallas_call x1, Pallas kernels, local(): call(out_kernel, [((NRHS, width), bf16)], ins=[VMEM] * 6, flops=2 * NRHS...  1.01 us
  transfers between devices with their start and end apart: 4, of which 1 were waited for; matrix products, arithmetic and copies ran while one was open for 0% of the time, Pallas kernels for 4%

profile of v6, /device:TPU:6, one launch (start us, length us, event | category | flops | bytes accessed | tf_op | source)
XLA Modules:
  0.0 34.7 jit_solution(3982550749024326277)
XLA Ops:
  0.0 4.9 %coeffs.1 = (bf16[16,256]{1,0:T(8,128)(2,1)S(1)}, bf16[256,128]{1,0:T(8,128)(2,1)}, bf16[16,640]{1,0:T(8,128)(2,1)S(1)}, bf16[16,640]{1,0:T(8,128)(2,1)S(1)}, bf...) custom-call(bf16[16,1024]{1,0:T(8,128)(2,1)} %refs_0_.1, ...), custom_call_target="tpu_custom_call" | custom-call | flops 2621440 | bytes 2097152 | tf_op jit(solution)/shard_map/coeffs/pallas_call | solution.py:328
  4.9 14.6 %all-to-all-start = ((bf16[32,8,128]{2,1,0:T(8,128)(2,1)}), bf16[32,8,128]{2,1,0:T(8,128)(2,1)S(1)}, u32[]{:S(2)}, u32[]{:S(2)}) async-start(bf16[32,8,128]{2,1,0:T(8,128)(2,1)} %bitcast), calls=%async_computation | async-start | bytes 131072 | tf_op jit(solution)/shard_map/all_to_all | solution.py:354
  19.4 3.3 %collective-permute-start.1 = (bf16[16,640]{1,0:T(8,128)(2,1)S(1)}, bf16[16,640]{1,0:T(8,128)(2,1)S(1)}, u32[]{:S(2)}, u32[]{:S(2)}) collective-permute-start(bf16[16,640]{1,0:T(8,128)(2,1)S(1)} %get-tuple-element.29), channel_id=1, source_target_pairs={{1,2},{2,1},{3,4},{4,3},{5,6},{6,5},{7,8},{8,7},{9,10},{10,9},{11,... | collective-permute-start | bytes 61448 | tf_op jit(solution)/shard_map/ppermute | solution.py:291
  22.8 3.4 %collective-permute-start.2 = (bf16[16,640]{1,0:T(8,128)(2,1)S(1)}, bf16[16,640]{1,0:T(8,128)(2,1)S(1)}, u32[]{:S(2)}, u32[]{:S(2)}) collective-permute-start(bf16[16,640]{1,0:T(8,128)(2,1)S(1)} %get-tuple-element.30), channel_id=1, source_target_pairs={{0,1},{1,0},{2,3},{3,2},{4,5},{5,4},{6,7},{7,6},{8,9},{9,8},{10,11... | collective-permute-start | bytes 61448 | tf_op jit(solution)/shard_map/ppermute | solution.py:291
  26.2 0.0 all-to-all-done
  26.2 0.4 %tree.1 = (f32[16,64]{1,0:T(8,128)S(1)}, f32[8,128]{1,0:T(8,128)S(1)}) custom-call(bf16[256,128]{1,0:T(8,128)(2,1)S(1)} %bitcast.2, bf16[2,2048,128]{2,1,0:T(8,128)(2,1)S(1)} %get-tuple-element.22.folded_ref, bf16[4,2,64,64]{3,2,1,0:T(8,128)(2,1)} %up_hbm.1, bf16[5,2,64,64]{3,2,1,0:T(8,128)(2,1)} %coup_hbm.1), custom_call_target="tpu_custom_call" | custom-call | flops 8388608 | bytes 262144 | tf_op jit(solution)/shard_map/tree/pallas_call | solution.py:372
  26.6 3.0 %collective-permute-start = (f32[8,128]{1,0:T(8,128)S(1)}, f32[8,128]{1,0:T(8,128)S(1)}, u32[]{:S(2)}, u32[]{:S(2)}) collective-permute-start(f32[8,128]{1,0:T(8,128)S(1)} %get-tuple-element.24), channel_id=1, source_target_pairs={{16,32},{32,16},{17,33},{33,17},{18,34},{34,18},{19,35},{35,19},{2... | collective-permute-start | bytes 12296 | tf_op jit(solution)/shard_map/ppermute | solution.py:284
  29.6 0.0 collective-permute-done.1.first_ref
  29.6 0.0 collective-permute-done.2.second_ref
  29.6 1.1 %near.1 = (f32[16,1024]{1,0:T(8,128)S(1)}, f32[16,256]{1,0:T(8,128)S(1)}, bf16[4,6,64,64]{3,2,1,0:T(8,128)(2,1)S(1)}, bf16[4,3,256,256]{3,2,1,0:T(8,128)(2,1)S(1)}) custom-call(s32[4,3]{1,0:T(4,128)S(1)} %get-tuple-element.25.near_src, s32[4,6]{1,0:T(4,128)S(1)} %get-tuple-element.26.coup_src, ...), custom_call_target="tpu_custom_call", output_to_operand_aliasing={{2}: (8, {}), {3}: (9, {})} | custom-call | flops 28311552 | bytes 2097152 | tf_op jit(solution)/shard_map/near/pallas_call | solution.py:357
  30.8 2.9 %collective-permute-done.cross_ref = f32[8,128]{1,0:T(8,128)S(1)} collective-permute-done((f32[8,128]{1,0:T(8,128)S(1)}, f32[8,128]{1,0:T(8,128)S(1)}, u32[]{:S(2)}, u32[]{:S(2)}) %collective-permute-start) | collective-permute-done | bytes 4128 | tf_op jit(solution)/shard_map/ppermute | solution.py:284
  33.7 1.0 %out.1 = bf16[16,1024]{1,0:T(8,128)(2,1)} custom-call(f32[16,64]{1,0:T(8,128)S(1)} %get-tuple-element.23.own_ref, f32[8,128]{1,0:T(8,128)S(1)} %collective-permute-done.cross_ref, f32[16,256]{1,0:T(8,128)S(1)} %get-tuple-element.33.field_ref, f32[16,1024]{1,0:T(8,128)S(1)} %get-tuple-element.34.near_ref, ...), custom_call_target="tpu_custom_call" | custom-call | flops 2621440 | bytes 262144 | tf_op jit(solution)/shard_map/out/pallas_call | solution.py:384
Async XLA Ops:
  4.9 21.3 %all-to-all-start = ((bf16[32,8,128]{2,1,0:T(8,128)(2,1)}), bf16[32,8,128]{2,1,0:T(8,128)(2,1)S(1)}, u32[]{:S(2)}, u32[]{:S(2)}) async-start(bf16[32,8,128]{2,1,0:T(8,128)(2,1)} %bitcast), calls=%async_computation | async-start | bytes 131072 | tf_op jit(solution)/shard_map/all_to_all | solution.py:354
  19.4 10.1 %collective-permute-start.1 = (bf16[16,640]{1,0:T(8,128)(2,1)S(1)}, bf16[16,640]{1,0:T(8,128)(2,1)S(1)}, u32[]{:S(2)}, u32[]{:S(2)}) collective-permute-start(bf16[16,640]{1,0:T(8,128)(2,1)S(1)} %get-tuple-element.29), channel_id=1, source_target_pairs={{1,2},{2,1},{3,4},{4,3},{5,6},{6,5},{7,8},{8,7},{9,10},{10,9},{11,... | collective-permute-start | bytes 61448 | tf_op jit(solution)/shard_map/ppermute | solution.py:291
  22.8 6.8 %collective-permute-start.2 = (bf16[16,640]{1,0:T(8,128)(2,1)S(1)}, bf16[16,640]{1,0:T(8,128)(2,1)S(1)}, u32[]{:S(2)}, u32[]{:S(2)}) collective-permute-start(bf16[16,640]{1,0:T(8,128)(2,1)S(1)} %get-tuple-element.30), channel_id=1, source_target_pairs={{0,1},{1,0},{2,3},{3,2},{4,5},{5,4},{6,7},{7,6},{8,9},{9,8},{10,11... | collective-permute-start | bytes 61448 | tf_op jit(solution)/shard_map/ppermute | solution.py:291
  26.6 7.0 %collective-permute-start = (f32[8,128]{1,0:T(8,128)S(1)}, f32[8,128]{1,0:T(8,128)S(1)}, u32[]{:S(2)}, u32[]{:S(2)}) collective-permute-start(f32[8,128]{1,0:T(8,128)S(1)} %get-tuple-element.24), channel_id=1, source_target_pairs={{16,32},{32,16},{17,33},{33,17},{18,34},{34,18},{19,35},{35,19},{2... | collective-permute-start | bytes 12296 | tf_op jit(solution)/shard_map/ppermute | solution.py:284

commit v7 on v6

--- a/solution.py
+++ b/solution.py
@@ -25,7 +25,7 @@
 STAGED = 5
 HELD = 2
 EARLY = 6
-FOLDED = 4
+FOLDED = 3
 NT = (((1,), (1,)), ((), ()))
 NN = (((1,), (0,)), ((), ()))
 TN = (((0,), (0,)), ((), ()))

time: 35 us -> 34.9 us (level)
  no operation moved by 1% of the time
where the time goes in v7:
time: 34.9 us; the launch traced here: 34.6 us
  starting transfers between devices  24.2 us (69%)
  Pallas kernels  7.44 us (21%)
  waiting for transfers between devices  2.91 us (8%)
    all_to_all x1, starting transfers between devices, local(): lax.all_to_all(sends, ('gy', 'gz'), 0, 0, tiled=True, axis_index_groups=p...  14.5 us
    ppermute x2, starting transfers between devices, traded(): return lax.ppermute(values, AXES, route)  6.74 us
    pallas_call x1, Pallas kernels, local(): call(coeff_kernel, [((NRHS, ranks), bf16), ((PAIR * 8, 2 * RANK), bf16),...  4.88 us
    ppermute x1, starting transfers between devices, crossed(): return lax.ppermute(values, AXES, route)  2.95 us
    ppermute x1, waiting for transfers between devices, crossed(): return lax.ppermute(values, AXES, route)  2.9 us
    pallas_call x1, Pallas kernels, local(): call(near_kernel, [((NRHS, width), f32), ((NRHS, ranks), f32)] + [(x.shap...  1.15 us
    pallas_call x1, Pallas kernels, local(): call(out_kernel, [((NRHS, width), bf16)], ins=[VMEM] * 6, flops=2 * NRHS...  1.01 us
  transfers between devices with their start and end apart: 4, of which 1 were waited for; matrix products, arithmetic and copies ran while one was open for 0% of the time, Pallas kernels for 4%

profile of v7, /device:TPU:6, one launch (start us, length us, event | category | flops | bytes accessed | tf_op | source)
XLA Modules:
  0.0 34.6 jit_solution(17334799735285183836)
XLA Ops:
  0.0 4.9 %coeffs.1 = (bf16[16,256]{1,0:T(8,128)(2,1)S(1)}, bf16[256,128]{1,0:T(8,128)(2,1)}, bf16[16,640]{1,0:T(8,128)(2,1)S(1)}, bf16[16,640]{1,0:T(8,128)(2,1)S(1)}, bf...) custom-call(bf16[16,1024]{1,0:T(8,128)(2,1)} %refs_0_.1, ...), custom_call_target="tpu_custom_call" | custom-call | flops 2621440 | bytes 2097152 | tf_op jit(solution)/shard_map/coeffs/pallas_call | solution.py:328
  4.9 14.5 %all-to-all-start = ((bf16[32,8,128]{2,1,0:T(8,128)(2,1)}), bf16[32,8,128]{2,1,0:T(8,128)(2,1)S(1)}, u32[]{:S(2)}, u32[]{:S(2)}) async-start(bf16[32,8,128]{2,1,0:T(8,128)(2,1)} %bitcast), calls=%async_computation | async-start | bytes 131072 | tf_op jit(solution)/shard_map/all_to_all | solution.py:354
  19.4 3.3 %collective-permute-start.1 = (bf16[16,640]{1,0:T(8,128)(2,1)S(1)}, bf16[16,640]{1,0:T(8,128)(2,1)S(1)}, u32[]{:S(2)}, u32[]{:S(2)}) collective-permute-start(bf16[16,640]{1,0:T(8,128)(2,1)S(1)} %get-tuple-element.29), channel_id=1, source_target_pairs={{1,2},{2,1},{3,4},{4,3},{5,6},{6,5},{7,8},{8,7},{9,10},{10,9},{11,... | collective-permute-start | bytes 61448 | tf_op jit(solution)/shard_map/ppermute | solution.py:291
  22.7 3.4 %collective-permute-start.2 = (bf16[16,640]{1,0:T(8,128)(2,1)S(1)}, bf16[16,640]{1,0:T(8,128)(2,1)S(1)}, u32[]{:S(2)}, u32[]{:S(2)}) collective-permute-start(bf16[16,640]{1,0:T(8,128)(2,1)S(1)} %get-tuple-element.30), channel_id=1, source_target_pairs={{0,1},{1,0},{2,3},{3,2},{4,5},{5,4},{6,7},{7,6},{8,9},{9,8},{10,11... | collective-permute-start | bytes 61448 | tf_op jit(solution)/shard_map/ppermute | solution.py:291
  26.1 0.0 all-to-all-done
  26.1 0.4 %tree.1 = (f32[16,64]{1,0:T(8,128)S(1)}, f32[8,128]{1,0:T(8,128)S(1)}) custom-call(bf16[256,128]{1,0:T(8,128)(2,1)S(1)} %bitcast.2, bf16[2,2048,128]{2,1,0:T(8,128)(2,1)S(1)} %get-tuple-element.22.folded_ref, bf16[4,2,64,64]{3,2,1,0:T(8,128)(2,1)} %up_hbm.1, bf16[5,2,64,64]{3,2,1,0:T(8,128)(2,1)} %coup_hbm.1), custom_call_target="tpu_custom_call" | custom-call | flops 8388608 | bytes 262144 | tf_op jit(solution)/shard_map/tree/pallas_call | solution.py:372
  26.6 2.9 %collective-permute-start = (f32[8,128]{1,0:T(8,128)S(1)}, f32[8,128]{1,0:T(8,128)S(1)}, u32[]{:S(2)}, u32[]{:S(2)}) collective-permute-start(f32[8,128]{1,0:T(8,128)S(1)} %get-tuple-element.24), channel_id=1, source_target_pairs={{16,32},{32,16},{17,33},{33,17},{18,34},{34,18},{19,35},{35,19},{2... | collective-permute-start | bytes 12296 | tf_op jit(solution)/shard_map/ppermute | solution.py:284
  29.5 0.0 collective-permute-done.1.first_ref
  29.5 0.0 collective-permute-done.2.second_ref
  29.5 1.1 %near.1 = (f32[16,1024]{1,0:T(8,128)S(1)}, f32[16,256]{1,0:T(8,128)S(1)}, bf16[4,6,64,64]{3,2,1,0:T(8,128)(2,1)S(1)}, bf16[4,3,256,256]{3,2,1,0:T(8,128)(2,1)S(1)}) custom-call(s32[4,3]{1,0:T(4,128)S(1)} %get-tuple-element.25.near_src, s32[4,6]{1,0:T(4,128)S(1)} %get-tuple-element.26.coup_src, ...), custom_call_target="tpu_custom_call", output_to_operand_aliasing={{2}: (8, {}), {3}: (9, {})} | custom-call | flops 28311552 | bytes 2097152 | tf_op jit(solution)/shard_map/near/pallas_call | solution.py:357
  30.7 2.9 %collective-permute-done.cross_ref = f32[8,128]{1,0:T(8,128)S(1)} collective-permute-done((f32[8,128]{1,0:T(8,128)S(1)}, f32[8,128]{1,0:T(8,128)S(1)}, u32[]{:S(2)}, u32[]{:S(2)}) %collective-permute-start) | collective-permute-done | bytes 4128 | tf_op jit(solution)/shard_map/ppermute | solution.py:284
  33.6 1.0 %out.1 = bf16[16,1024]{1,0:T(8,128)(2,1)} custom-call(f32[16,64]{1,0:T(8,128)S(1)} %get-tuple-element.23.own_ref, f32[8,128]{1,0:T(8,128)S(1)} %collective-permute-done.cross_ref, f32[16,256]{1,0:T(8,128)S(1)} %get-tuple-element.33.field_ref, f32[16,1024]{1,0:T(8,128)S(1)} %get-tuple-element.34.near_ref, ...), custom_call_target="tpu_custom_call" | custom-call | flops 2621440 | bytes 262144 | tf_op jit(solution)/shard_map/out/pallas_call | solution.py:384
Async XLA Ops:
  4.9 21.3 %all-to-all-start = ((bf16[32,8,128]{2,1,0:T(8,128)(2,1)}), bf16[32,8,128]{2,1,0:T(8,128)(2,1)S(1)}, u32[]{:S(2)}, u32[]{:S(2)}) async-start(bf16[32,8,128]{2,1,0:T(8,128)(2,1)} %bitcast), calls=%async_computation | async-start | bytes 131072 | tf_op jit(solution)/shard_map/all_to_all | solution.py:354
  19.4 10.1 %collective-permute-start.1 = (bf16[16,640]{1,0:T(8,128)(2,1)S(1)}, bf16[16,640]{1,0:T(8,128)(2,1)S(1)}, u32[]{:S(2)}, u32[]{:S(2)}) collective-permute-start(bf16[16,640]{1,0:T(8,128)(2,1)S(1)} %get-tuple-element.29), channel_id=1, source_target_pairs={{1,2},{2,1},{3,4},{4,3},{5,6},{6,5},{7,8},{8,7},{9,10},{10,9},{11,... | collective-permute-start | bytes 61448 | tf_op jit(solution)/shard_map/ppermute | solution.py:291
  22.7 6.8 %collective-permute-start.2 = (bf16[16,640]{1,0:T(8,128)(2,1)S(1)}, bf16[16,640]{1,0:T(8,128)(2,1)S(1)}, u32[]{:S(2)}, u32[]{:S(2)}) collective-permute-start(bf16[16,640]{1,0:T(8,128)(2,1)S(1)} %get-tuple-element.30), channel_id=1, source_target_pairs={{0,1},{1,0},{2,3},{3,2},{4,5},{5,4},{6,7},{7,6},{8,9},{9,8},{10,11... | collective-permute-start | bytes 61448 | tf_op jit(solution)/shard_map/ppermute | solution.py:291
  26.6 7.0 %collective-permute-start = (f32[8,128]{1,0:T(8,128)S(1)}, f32[8,128]{1,0:T(8,128)S(1)}, u32[]{:S(2)}, u32[]{:S(2)}) collective-permute-start(f32[8,128]{1,0:T(8,128)S(1)} %get-tuple-element.24), channel_id=1, source_target_pairs={{16,32},{32,16},{17,33},{33,17},{18,34},{34,18},{19,35},{35,19},{2... | collective-permute-start | bytes 12296 | tf_op jit(solution)/shard_map/ppermute | solution.py:284
